TPU v7x, 32 devices: a whole 2x2x4 slice. The times are simulated.
32 devices in a mesh: clip: 8 (over y, x, core), seq: 4 (over z).
Axes of the slice: x: 2, y: 2, z: 4, core: 2. Of those that a mesh axis runs over, the one named last changes fastest.
Arguments:
- tokens: bfloat16 [32, 380, 768], P('clip', 'seq'), may hold values from -6 to 6
- freq_index: int32 [32, 7], P('clip'), may hold values from 0 to 11, as said below
- time_index: int32 [32, 54], P('clip'), may hold values from 0 to 98, as said below
- freq_table: bfloat16 [12, 768], replicated, may hold values from -3 to 3
- time_table: bfloat16 [99, 768], replicated, may hold values from -3 to 3
- norm1_gain: bfloat16 [768], replicated, may hold values from 0.25 to 1.75
- norm1_shift: bfloat16 [768], replicated, may hold values from -2 to 2
- qkv_weight: bfloat16 [768, 2304], replicated, may hold values from -0.21875 to 0.21875
- qv_bias: bfloat16 [2, 768], replicated, may hold values from -2 to 2
- proj_weight: bfloat16 [768, 768], replicated, may hold values from -2.5 to 2.5
- proj_bias: bfloat16 [768], replicated, may hold values from -2 to 2
- norm2_gain: bfloat16 [768], replicated, may hold values from 0.25 to 1.75
- norm2_shift: bfloat16 [768], replicated, may hold values from -2 to 2
- fc1_weight: bfloat16 [768, 3072], replicated, may hold values from -0.21875 to 0.21875
- fc1_bias: bfloat16 [3072], replicated, may hold values from -3 to 3
- fc2_weight: bfloat16 [3072, 768], replicated, may hold values from -0.15625 to 0.15625
- fc2_bias: bfloat16 [768], replicated, may hold values from -2 to 2
- cotangent: bfloat16 [32, 380, 768], P('clip', 'seq'), may hold values from -6 to 6
Outputs:
- block_out: bfloat16 [32, 380, 768], P('clip', 'seq')
- input_grad: bfloat16 [32, 380, 768], P('clip', 'seq')
- freq_table_grad: float32 [12, 768], replicated
- time_table_grad: float32 [99, 768], replicated
- norm1_gain_grad: float32 [768], replicated
- norm1_shift_grad: float32 [768], replicated
- qkv_weight_grad: float32 [768, 2304], P('clip')
- qv_bias_grad: float32 [2, 768], replicated
- proj_weight_grad: float32 [768, 768], P('clip')
- proj_bias_grad: float32 [768], replicated
- norm2_gain_grad: float32 [768], replicated
- norm2_shift_grad: float32 [768], replicated
- fc1_weight_grad: float32 [768, 3072], P('clip')
- fc1_bias_grad: float32 [3072], replicated
- fc2_weight_grad: float32 [3072, 768], P('clip')
- fc2_bias_grad: float32 [768], replicated
Inputs may be any that keep to these rules, and one draw needn't show every extreme that they name: `freq_index`: each clip's 7 frequency rows are distinct and increasing. `time_index`: each clip's 54 time columns are distinct and increasing.
All inputs are finite; a program needn't handle non-finite values.
Results may differ from a plain program's by a relative error of at most 0.012.
Values may be sent and summed in bfloat16 or wider, within the bound.
A program may use at most 192 MiB of HBM per device.

v0:
```python
import jax
import jax.numpy as jnp
from jax import lax
from jax.sharding import PartitionSpec as P

HDIM = 64
FKEEP = 7
TKEEP = 54


def layer_norm(values, gain_vec, offset_vec):
    row_mean = jnp.mean(values, -1, keepdims=True)
    centered = values - row_mean
    variance = jnp.mean(centered * centered, -1, keepdims=True)
    return centered * lax.rsqrt(variance + 1e-06) * gain_vec + offset_vec


def gelu_exact(values):
    return jax.nn.gelu(values, approximate=False)


def attend(piece):
    items, row_count, lane_width = (piece.shape[0], piece.shape[1], piece.shape[4])
    by_head = piece.reshape(items, row_count, 3, lane_width // HDIM, HDIM)
    scores = jnp.einsum(
        "nqhe,nkhe->nhqk", by_head[:, :, 0], by_head[:, :, 1], preferred_element_type=jnp.float32
    ) * HDIM ** (-0.5)
    row_max = jnp.max(scores, -1, keepdims=True)
    exponent = jnp.exp(scores - row_max)
    attn_probs = exponent / jnp.sum(exponent, -1, keepdims=True)
    attended = jnp.einsum(
        "nhqk,nkhe->nqhe",
        attn_probs.astype(jnp.bfloat16),
        by_head[:, :, 2],
        preferred_element_type=jnp.float32,
    )
    attended = attended.astype(jnp.bfloat16).reshape(items, row_count, 1, lane_width)
    return (attended, attn_probs, piece)


def attend_back(head_blocks, attn_probs, grad_heads):
    items, row_count, lane_width = (
        head_blocks.shape[0],
        head_blocks.shape[1],
        head_blocks.shape[4],
    )
    by_head = head_blocks.reshape(items, row_count, 3, lane_width // HDIM, HDIM)
    query_part, key_part, value_part = (by_head[:, :, 0], by_head[:, :, 1], by_head[:, :, 2])
    grad_out = grad_heads.reshape(items, row_count, lane_width // HDIM, HDIM)
    grad_probs = jnp.einsum(
        "nqhe,nkhe->nhqk", grad_out, value_part, preferred_element_type=jnp.float32
    )
    row_inner = jnp.sum(grad_probs * attn_probs, -1, keepdims=True)
    grad_scores = (attn_probs * (grad_probs - row_inner)).astype(jnp.bfloat16)
    scale_value = HDIM ** (-0.5)
    grad_query = (
        jnp.einsum("nhqk,nkhe->nqhe", grad_scores, key_part, preferred_element_type=jnp.float32)
        * scale_value
    )
    grad_key = (
        jnp.einsum("nhqk,nqhe->nkhe", grad_scores, query_part, preferred_element_type=jnp.float32)
        * scale_value
    )
    grad_value = jnp.einsum(
        "nhqk,nqhe->nkhe",
        attn_probs.astype(jnp.bfloat16),
        grad_out,
        preferred_element_type=jnp.float32,
    )
    stacked = jnp.stack([grad_query, grad_key, grad_value], 2).astype(jnp.bfloat16)
    return stacked.reshape(items, row_count, 3, 1, lane_width)


def positions(freq_index, time_index, freq_count, time_count, row_local):
    global_row = lax.axis_index("seq") * row_local + jnp.arange(row_local, dtype=jnp.int32)
    patch_number = jnp.maximum(global_row - 2, 0)
    is_patch = (global_row >= 2)[None, :, None]
    freq_slot = ((patch_number // TKEEP)[:, None] == jnp.arange(FKEEP, dtype=jnp.int32)).astype(
        jnp.int32
    )
    time_slot = ((patch_number % TKEEP)[:, None] == jnp.arange(TKEEP, dtype=jnp.int32)).astype(
        jnp.int32
    )
    freq_pick = jnp.sum(freq_slot[None] * freq_index[:, None, :], -1)
    time_pick = jnp.sum(time_slot[None] * time_index[:, None, :], -1)
    freq_hot = (freq_pick[..., None] == jnp.arange(freq_count, dtype=jnp.int32)) & is_patch
    time_hot = (time_pick[..., None] == jnp.arange(time_count, dtype=jnp.int32)) & is_patch
    return (
        freq_hot.astype(jnp.bfloat16).reshape(-1, freq_count),
        time_hot.astype(jnp.bfloat16).reshape(-1, time_count),
    )


def forward(tokens, position, params):
    (
        norm1_gain,
        norm1_shift,
        qkv_weight,
        qv_bias,
        proj_weight,
        proj_bias,
        norm2_gain,
        norm2_shift,
        fc1_weight,
        fc1_bias,
        fc2_weight,
        fc2_bias,
    ) = params
    clip_count, row_local, model_width = tokens.shape
    groups = lax.axis_size("seq")
    stream_in = tokens.reshape(-1, model_width).astype(jnp.float32) + position
    normed_first = layer_norm(
        stream_in, norm1_gain.astype(jnp.float32), norm1_shift.astype(jnp.float32)
    ).astype(jnp.bfloat16)
    bias_full = jnp.concatenate([qv_bias[0], jnp.zeros_like(qv_bias[0]), qv_bias[1]]).astype(
        jnp.float32
    )
    projected = (
        jnp.dot(normed_first, qkv_weight, preferred_element_type=jnp.float32) + bias_full
    ).astype(jnp.bfloat16)
    sending = projected.reshape(clip_count, row_local, 3, groups, model_width // groups)
    attended, attn_probs, head_blocks = attend(
        lax.all_to_all(sending, "seq", split_axis=3, concat_axis=1, tiled=True)
    )
    back_rows = lax.all_to_all(attended, "seq", split_axis=1, concat_axis=2, tiled=True).reshape(
        -1, model_width
    )
    stream_mid = stream_in + (
        jnp.dot(back_rows, proj_weight, preferred_element_type=jnp.float32)
        + proj_bias.astype(jnp.float32)
    )
    normed_second = layer_norm(
        stream_mid, norm2_gain.astype(jnp.float32), norm2_shift.astype(jnp.float32)
    ).astype(jnp.bfloat16)
    hidden = jnp.dot(
        normed_second, fc1_weight, preferred_element_type=jnp.float32
    ) + fc1_bias.astype(jnp.float32)
    activated = gelu_exact(hidden).astype(jnp.bfloat16)
    block_out = stream_mid + (
        jnp.dot(activated, fc2_weight, preferred_element_type=jnp.float32)
        + fc2_bias.astype(jnp.float32)
    )
    return (
        stream_in,
        normed_first,
        head_blocks,
        attn_probs,
        back_rows,
        stream_mid,
        normed_second,
        hidden,
        activated,
        block_out,
    )


def on_device(
    tokens,
    freq_index,
    time_index,
    freq_table,
    time_table,
    norm1_gain,
    norm1_shift,
    qkv_weight,
    qv_bias,
    proj_weight,
    proj_bias,
    norm2_gain,
    norm2_shift,
    fc1_weight,
    fc1_bias,
    fc2_weight,
    fc2_bias,
    cotangent,
):
    params = (
        norm1_gain,
        norm1_shift,
        qkv_weight,
        qv_bias,
        proj_weight,
        proj_bias,
        norm2_gain,
        norm2_shift,
        fc1_weight,
        fc1_bias,
        fc2_weight,
        fc2_bias,
    )
    clip_count, row_local, model_width = tokens.shape
    groups = lax.axis_size("seq")
    freq_hot, time_hot = positions(
        freq_index, time_index, freq_table.shape[0], time_table.shape[0], row_local
    )
    position = jnp.dot(freq_hot, freq_table, preferred_element_type=jnp.float32) + jnp.dot(
        time_hot, time_table, preferred_element_type=jnp.float32
    )
    first_pass = forward(tokens, position, params)
    tokens_again, position_again, params_again = lax.optimization_barrier(
        (tokens, position, params)
    )
    stored = forward(tokens_again, position_again, params_again)
    (
        stream_in,
        normed_first,
        head_blocks,
        attn_probs,
        back_rows,
        stream_mid,
        normed_second,
        hidden,
        activated,
        unused_out,
    ) = stored
    grad_mlp = cotangent.reshape(-1, model_width)
    fc2_grad = jnp.einsum("mf,md->fd", activated, grad_mlp, preferred_element_type=jnp.float32)
    fc2_bias_grad = jnp.sum(grad_mlp, 0, dtype=jnp.float32)
    grad_act = jnp.einsum("md,fd->mf", grad_mlp, fc2_weight, preferred_element_type=jnp.float32)
    unused_gelu, gelu_pull = jax.vjp(gelu_exact, hidden)
    grad_hidden = gelu_pull(grad_act)[0].astype(jnp.bfloat16)
    fc1_grad = jnp.einsum(
        "md,mf->df", normed_second, grad_hidden, preferred_element_type=jnp.float32
    )
    fc1_bias_grad = jnp.sum(grad_hidden, 0, dtype=jnp.float32)
    grad_second = jnp.einsum(
        "mf,df->md", grad_hidden, fc1_weight, preferred_element_type=jnp.float32
    )
    unused_second, second_pull = jax.vjp(
        layer_norm, stream_mid, norm2_gain.astype(jnp.float32), norm2_shift.astype(jnp.float32)
    )
    grad_mid_norm, norm2_gain_grad, norm2_shift_grad = second_pull(grad_second)
    grad_mid = grad_mlp.astype(jnp.float32) + grad_mid_norm
    grad_branch = grad_mid.astype(jnp.bfloat16)
    proj_grad = jnp.einsum("md,me->de", back_rows, grad_branch, preferred_element_type=jnp.float32)
    proj_bias_grad = jnp.sum(grad_branch, 0, dtype=jnp.float32)
    grad_att = jnp.einsum(
        "me,de->md", grad_branch, proj_weight, preferred_element_type=jnp.float32
    ).astype(jnp.bfloat16)
    grad_send = grad_att.reshape(clip_count, row_local, groups, model_width // groups)
    grad_heads = lax.all_to_all(grad_send, "seq", split_axis=2, concat_axis=1, tiled=True)
    grad_qkv_heads = attend_back(head_blocks, attn_probs, grad_heads)
    grad_rows = lax.all_to_all(
        grad_qkv_heads, "seq", split_axis=1, concat_axis=3, tiled=True
    ).reshape(-1, 3 * model_width)
    qkv_grad = jnp.einsum("md,me->de", normed_first, grad_rows, preferred_element_type=jnp.float32)
    column_sums = jnp.sum(grad_rows, 0, dtype=jnp.float32)
    qv_bias_grad = jnp.stack([column_sums[:model_width], column_sums[2 * model_width :]])
    grad_first = jnp.einsum("me,de->md", grad_rows, qkv_weight, preferred_element_type=jnp.float32)
    unused_first, first_pull = jax.vjp(
        layer_norm, stream_in, norm1_gain.astype(jnp.float32), norm1_shift.astype(jnp.float32)
    )
    grad_in_norm, norm1_gain_grad, norm1_shift_grad = first_pull(grad_first)
    grad_in = grad_mid + grad_in_norm
    freq_grad = jnp.dot(freq_hot.astype(jnp.float32).T, grad_in, precision=lax.Precision.HIGHEST)
    time_grad = jnp.dot(time_hot.astype(jnp.float32).T, grad_in, precision=lax.Precision.HIGHEST)
    matrices = (qkv_grad, proj_grad, fc1_grad, fc2_grad)
    shares = (
        lax.psum_scatter(matrices[0], "clip", scatter_dimension=0, tiled=True),
        lax.psum_scatter(matrices[1], "clip", scatter_dimension=0, tiled=True),
        lax.psum_scatter(matrices[2], "clip", scatter_dimension=0, tiled=True),
        lax.psum_scatter(matrices[3], "clip", scatter_dimension=0, tiled=True),
    )
    shares = lax.psum((shares[0], shares[1], shares[2], shares[3]), "seq")
    small_grads = lax.psum(
        (
            freq_grad,
            time_grad,
            norm1_gain_grad,
            norm1_shift_grad,
            qv_bias_grad,
            proj_bias_grad,
            norm2_gain_grad,
            norm2_shift_grad,
            fc1_bias_grad,
            fc2_bias_grad,
        ),
        ("clip", "seq"),
    )
    block_out = first_pass[9].astype(jnp.bfloat16).reshape(tokens.shape)
    input_grad = grad_in.astype(jnp.bfloat16).reshape(tokens.shape)
    return (
        block_out,
        input_grad,
        small_grads[0],
        small_grads[1],
        small_grads[2],
        small_grads[3],
        shares[0],
        small_grads[4],
        shares[1],
        small_grads[5],
        small_grads[6],
        small_grads[7],
        shares[2],
        small_grads[8],
        shares[3],
        small_grads[9],
    )


def solution(mesh):
    in_specs = (
        P("clip", "seq", None),
        P("clip", None),
        P("clip", None),
        P(),
        P(),
        P(),
        P(),
        P(),
        P(),
        P(),
        P(),
        P(),
        P(),
        P(),
        P(),
        P(),
        P(),
        P("clip", "seq", None),
    )
    out_specs = (
        P("clip", "seq", None),
        P("clip", "seq", None),
        P(),
        P(),
        P(),
        P(),
        P("clip", None),
        P(),
        P("clip", None),
        P(),
        P(),
        P(),
        P("clip", None),
        P(),
        P("clip", None),
        P(),
    )
    return jax.shard_map(
        on_device, mesh=mesh, in_specs=in_specs, out_specs=out_specs, check_vma=False
    )
```

profile of v0, /device:TPU:0, one launch (start us, length us, event | category | flops | bytes accessed | tf_op | source)
XLA Modules:
  0.0 973.5 jit_solution(11992144282609343915)
XLA Ops:
  19.1 2.4 reshape.374
  23.3 3.7 fusion.162
  28.2 2.4 reshape.375
  34.1 2.9 fusion.25
  37.0 5.7 reshape.366
  42.7 2.6 copy.189
  45.3 59.5 %all_to_all.90 = bf16[4,95,3,4,192]{4,0,2,1,3:T(4,128)(2,1)} all-to-all(bf16[4,95,3,4,192]{4,0,2,1,3:T(4,128)(2,1)S(1)} %copy.189), channel_id=1, replica_groups=mesh['clip'=8,'seq'=4] {'seq'}, dimensions={3} | all-to-all | bytes 3502080 | tf_op jit(solution)/shard_map/all_to_all | solution.py:123
  104.8 9.4 reshape.377
  114.2 4.5 fusion.163
  118.7 3.5 copy.228
  122.2 3.5 copy.229
  125.8 3.5 copy.227
  129.3 7.1 fusion.176
  136.3 4.6 fusion.42
  143.1 4.4 all-to-all-start.3
  154.7 12.0 %all-to-all-done.3 = bf16[4,380,1,192]{3,0,2,1:T(4,128)(2,1)} async-done(((bf16[4,380,1,192]{3,0,2,1:T(4,128)(2,1)}), bf16[4,380,1,192]{3,0,2,1:T(4,128)(2,1)}, u32[]{:S(2)}, u32[]{:S(2)}) %all-to-all-start.3) | async-done | bytes 583712 | tf_op jit(solution)/shard_map/all_to_all | solution.py:125
  166.7 2.4 copy.218
  169.1 2.6 copy.197
  171.6 2.6 reshape.369
  174.3 2.7 fusion.185
  177.3 4.6 convolution_add_fusion.2
  182.0 14.9 %convert_reduce_fusion = (f32[3072]{0:T(1024)}, bf16[380,3072]{1,0:T(8,128)(2,1)S(1)}, f32[380,3072]{1,0:T(8,128)}) fusion(f32[380,3072]{1,0:T(8,128)S(1)} %convolution_add_fusion.2, bf16[380,768]{1,0:T(8,128)(2,1)S(1)} %copy-done.9, bf16[3072,768]{1,0:T(8,128)(2,1)S(1)} %bitcast.147), kind=kOutput, calls=%fused_computation.18 | convolution fusion | flops 1879446528 | bytes 16988160 | tf_op jit(solution)/shard_map/md,fd->mf/dot_general | solution.py:219
  196.9 2.8 multiply_reduce_fusion.3
  204.5 2.9 reshape.370
  209.8 4.2 all-to-all-start.4
  214.0 3.5 fusion.186
  217.8 15.7 %all-to-all-done.4 = bf16[4,95,4,192]{3,0,1,2:T(4,128)(2,1)} async-done(((bf16[4,95,4,192]{3,0,1,2:T(4,128)(2,1)}), bf16[4,95,4,192]{3,0,1,2:T(4,128)(2,1)}, u32[]{:S(2)}, u32[]{:S(2)}) %all-to-all-start.4) | async-done | bytes 583712 | tf_op jit(solution)/shard_map/all_to_all | solution.py:241
  233.4 2.4 copy.199
  235.8 2.5 reshape.371
  238.3 7.8 multiply_reduce_fusion
  246.2 5.2 fusion.45
  251.4 6.5 multiply_convert_fusion
  268.2 3.0 pad_maximum_fusion
  271.3 55.5 %all_to_all.91 = bf16[4,380,3,1,192]{4,0,3,2,1:T(4,128)(2,1)} all-to-all(bf16[4,380,3,1,192]{4,0,3,2,1:T(4,128)(2,1)S(1)} %pad_maximum_fusion), channel_id=1, replica_groups=mesh['clip'=8,'seq'=4] {'seq'}, dimensions={1} | all-to-all | bytes 3502080 | tf_op jit(solution)/shard_map/all_to_all | solution.py:243
  326.8 5.7 copy.219
  332.5 6.0 copy.207
  338.5 5.0 reshape.372
  343.6 7.0 fusion.154
  351.0 11.4 %fusion.29 = f32[3072,768]{1,0:T(8,128)} fusion(bf16[380,768]{1,0:T(8,128)(2,1)} %reshape.365, f32[380,3072]{1,0:T(8,128)} %get-tuple-element.161, f32[380,3072]{1,0:T(8,128)} %copy-done.5), kind=kOutput, calls=%fused_computation.58 | convolution fusion | flops 1796567040 | bytes 19359744 | tf_op jit(solution)/shard_map/mf,md->fd/dot_general | solution.py:217
  363.2 8.7 fusion.155
  375.9 4.1 fusion.24
  380.0 5.7 reshape.360
  385.8 2.6 copy.178
  388.3 55.8 %all_to_all.92 = bf16[4,95,3,4,192]{4,0,2,1,3:T(4,128)(2,1)} all-to-all(bf16[4,95,3,4,192]{4,0,2,1,3:T(4,128)(2,1)S(1)} %copy.178), channel_id=1, replica_groups=mesh['clip'=8,'seq'=4] {'seq'}, dimensions={3} | all-to-all | bytes 3502080 | tf_op jit(solution)/shard_map/all_to_all | solution.py:123
  444.1 9.5 reshape.376
  453.6 4.7 fusion.164
  458.3 3.5 copy.225
  461.9 3.5 copy.226
  465.4 3.5 copy.224
  468.9 7.1 fusion.166
  476.0 4.7 fusion.48
  482.9 4.2 all-to-all-start.1
  492.9 13.2 %all-to-all-done.1 = bf16[4,380,1,192]{3,0,2,1:T(4,128)(2,1)} async-done(((bf16[4,380,1,192]{3,0,2,1:T(4,128)(2,1)}), bf16[4,380,1,192]{3,0,2,1:T(4,128)(2,1)}, u32[]{:S(2)}, u32[]{:S(2)}) %all-to-all-start.1) | async-done | bytes 583712 | tf_op jit(solution)/shard_map/all_to_all | solution.py:125
  506.1 2.5 copy.217
  508.6 2.7 copy.186
  511.2 2.7 reshape.363
  514.0 2.8 fusion.175
  525.4 4.2 multiply_reduce_fusion.4
  534.5 2.8 fusion.101
  538.3 37.4 %reduce-scatter.9.cloned.1.call-done = f32[96,3072]{1,0:T(8,128)} async-done(((f32[768,3072]{1,0:T(8,128)}), f32[96,3072]{1,0:T(8,128)}) %reduce-scatter.9.cloned.1.call-update) | async-done | bytes 1179664 | tf_op jit(solution)/shard_map/reduce_scatter | solution.py:261
  575.7 18.5 %fusion.49 = bf16[380,768]{1,0:T(8,128)(2,1)} fusion(f32[380,768]{1,0:T(8,128)} %copy-done.11, bf16[3072,768]{1,0:T(8,128)(2,1)} %param.33, bf16[768,3072]{1,0:T(8,128)(2,1)} %param.31, f32[3072]{0:T(1024)} %convert_element_type.187, f32[768]{0:T(1024)} %convert_element_type.189, f32[768]{0:T(1024)} %convert_element_type.185, f32[768]{0:T(1024)S(1)} %copy-done.41, ...), kind=kOutput, calls=%fused_computation.83 | convolution fusion | flops 3665510400 | bytes 11212768 | tf_op jit(solution)/shard_map/dot_general | solution.py:140
  603.0 73.7 %all-reduce.8.cloned.1.call-done = (f32[12,768]{1,0:T(8,128)}, f32[768]{0:T(1024)}, f32[768]{0:T(1024)}, f32[2,768]{1,0:T(2,128)}, f32[768]{0:T(1024)}, /*index=...) async-done(((f32[12,768]{1,0:T(8,128)}, f32[768]{0:T(1024)}, f32[768]{0:T(1024)}, f32[2,768]{1,0:T(2,128)}, f32[768]{0:T(1024)}, /*index=5*/f32[768]{0:T(1024)}, ...) | async-done | bytes 73744 | tf_op jit(solution)/shard_map/psum | solution.py:265
  676.6 133.0 %all-reduce.6.cloned.1.call-done = f32[99,768]{1,0:T(8,128)} async-done(((f32[99,768]{1,0:T(8,128)}), f32[99,768]{1,0:T(8,128)}) %all-reduce.6.cloned.1.call-update) | async-done | bytes 304144 | tf_op jit(solution)/shard_map/psum | solution.py:265
  809.6 138.1 %all-reduce.10.cloned.1.call-done = (f32[96,2304]{1,0:T(8,128)}, f32[96,768]{1,0:T(8,128)}, f32[96,3072]{1,0:T(8,128)}, f32[384,768]{1,0:T(8,128)}) async-done(((f32[96,2304]{1,0:T(8,128)}, f32[96,768]{1,0:T(8,128)}, f32[96,3072]{1,0:T(8,128)}, f32[384,768]{1,0:T(8,128)}), (f32[96,2304]{1,0:T(8,128)}, f32[96,768]{1,0:T(8,128)}, f32[96,3072]{1,0:T(8,128)}, ...) | async-done | bytes 3538960 | tf_op jit(solution)/shard_map/psum | solution.py:264
  (230 shorter events, 99.0 us)
Async XLA Ops:
  8.0 26.1 %copy-start = (bf16[768,2304]{1,0:T(8,128)(2,1)S(1)}, bf16[768,2304]{1,0:T(8,128)(2,1)}, u32[]{:S(2)}) copy-start(bf16[768,2304]{1,0:T(8,128)(2,1)} %param.25) | copy-start | bytes 10616836
  8.0 13.5 %copy-start.27 = (bf16[2,768]{1,0:T(2,128)(2,1)S(1)}, bf16[2,768]{1,0:T(2,128)(2,1)}, u32[]{:S(2)}) copy-start(bf16[2,768]{1,0:T(2,128)(2,1)} %param.26) | copy-start | bytes 9220
  9.8 17.2 %copy-start.45 = (pred[380]{0:T(512)(128)(4,1)}, pred[380]{0:T(512)(128)(4,1)S(1)}, u32[]{:S(2)}) copy-start(pred[380]{0:T(512)(128)(4,1)S(1)} %and.41) | copy-start | bytes 1144
  12.0 15.0 %copy-start.34 = (s32[380]{0:T(512)}, s32[380]{0:T(512)S(1)}, u32[]{:S(2)}) copy-start(s32[380]{0:T(512)S(1)} %eq.71) | copy-start | bytes 4564
  16.9 10.1 %copy-start.32 = (s32[380]{0:T(512)}, s32[380]{0:T(512)S(1)}, u32[]{:S(2)}) copy-start(s32[380]{0:T(512)S(1)} %eq.78) | copy-start | bytes 4564
  21.5 5.5 copy-start.17
  28.2 5.3 copy-start.50
  30.6 2.9 copy-start.51
  30.6 2.9 copy-start.53
  30.6 2.9 copy-start.54
  32.5 1.6 copy-start.1
  32.5 1.6 copy-start.23
  32.8 4.2 copy-start.28
  136.3 11.2 %copy-start.49 = (bf16[768]{0:T(1024)(128)(2,1)S(1)}, bf16[768]{0:T(1024)(128)(2,1)}, u32[]{:S(2)}) copy-start(bf16[768]{0:T(1024)(128)(2,1)} %param.29) | copy-start | bytes 4612
  136.3 11.8 %copy-start.52 = (bf16[768]{0:T(1024)(128)(2,1)S(1)}, bf16[768]{0:T(1024)(128)(2,1)}, u32[]{:S(2)}) copy-start(bf16[768]{0:T(1024)(128)(2,1)} %param.28) | copy-start | bytes 4612
  143.1 23.5 %all-to-all-start.3 = ((bf16[4,380,1,192]{3,0,2,1:T(4,128)(2,1)}), bf16[4,380,1,192]{3,0,2,1:T(4,128)(2,1)}, u32[]{:S(2)}, u32[]{:S(2)}) async-start(bf16[4,380,1,192]{3,0,2,1:T(4,128)(2,1)} %copy.195), calls=%async_computation.3 | async-start | bytes 1556480 | tf_op jit(solution)/shard_map/all_to_all | solution.py:125
  174.3 3.0 copy-start.44
  174.3 7.6 slice-start
  176.9 22.8 %copy-start.4 = (f32[380,768]{1,0:T(8,128)}, f32[380,768]{1,0:T(8,128)S(1)}, u32[]{:S(2)}) copy-start(f32[380,768]{1,0:T(8,128)S(1)} %get-tuple-element.192) | copy-start | bytes 3502084
  177.0 22.8 %copy-start.21 = (f32[380]{0:T(512)}, f32[380]{0:T(512)S(1)}, u32[]{:S(2)}) copy-start(f32[380]{0:T(512)S(1)} %broadcast_multiply_fusion) | copy-start | bytes 4564
  177.3 22.5 %copy-start.25 = (f32[380]{0:T(512)}, f32[380]{0:T(512)S(1)}, u32[]{:S(2)}) copy-start(f32[380]{0:T(512)S(1)} %fusion.119) | copy-start | bytes 4564
  177.3 4.6 copy-start.9
  177.3 4.6 slice-start.1
  177.3 19.6 %slice-start.2 = ((s8[4718592]{0:T(1024)(128)(4,1)}), s8[4194304]{0:T(1024)(128)(4,1)S(1)}, s32[]{:S(2)}) async-start(s8[4718592]{0:T(1024)(128)(4,1)} %bitcast.148), calls=%async_computation.19 | async-start | bytes 8388608
  181.9 15.0 %copy-start.5 = (f32[380,3072]{1,0:T(8,128)}, f32[380,3072]{1,0:T(8,128)S(1)}, u32[]{:S(2)}) copy-start(f32[380,3072]{1,0:T(8,128)S(1)} %convolution_add_fusion.2) | copy-start | bytes 14008324
  181.9 15.0 %copy-start.40 = (f32[768]{0:T(1024)S(1)}, f32[768]{0:T(1024)}, u32[]{:S(2)}) copy-start(f32[768]{0:T(1024)} %convert_element_type.184) | copy-start | bytes 9220
  181.9 15.0 %slice-start.3 = ((s8[4718592]{0:T(1024)(128)(4,1)}), s8[524288]{0:T(1024)(128)(4,1)S(1)}, s32[]{:S(2)}) async-start(s8[4718592]{0:T(1024)(128)(4,1)} %bitcast.148), calls=%async_computation.20 | async-start | bytes 1048576
  196.9 2.9 copy-start.16
  199.8 3.3 copy-start.12
  200.3 1.0 copy-start.7
  200.3 1.9 copy-start.38
  209.8 23.7 %all-to-all-start.4 = ((bf16[4,95,4,192]{3,0,1,2:T(4,128)(2,1)}), bf16[4,95,4,192]{3,0,1,2:T(4,128)(2,1)}, u32[]{:S(2)}, u32[]{:S(2)}) async-start(bf16[4,95,4,192]{3,0,1,2:T(4,128)(2,1)} %copy.198), calls=%async_computation.4 | async-start | bytes 1556480 | tf_op jit(solution)/shard_map/all_to_all | solution.py:241
  214.0 324.3 %reduce-scatter.7.cloned.1.call-start = ((), (), s32[]{:S(2)}) async-start(), calls=%async_computation.12 | async-start | bytes 2654208 | tf_op jit(solution)/shard_map/reduce_scatter | solution.py:260
  217.5 320.8 %reduce-scatter.5.cloned.1.call-start = ((), (), s32[]{:S(2)}) async-start(), calls=%async_computation.11 | async-start | bytes 7962624 | tf_op jit(solution)/shard_map/reduce_scatter | solution.py:259
  238.3 7.9 copy-start.20
  238.3 7.9 copy-start.30
  251.4 6.5 copy-start.14
  257.9 1.6 copy-start.13
  350.6 187.7 %reduce-scatter.11.cloned.1.call-start = ((), (), s32[]{:S(2)}) async-start(), calls=%async_computation.14 | async-start | bytes 10616832 | tf_op jit(solution)/shard_map/reduce_scatter | solution.py:262
  362.5 213.2 %reduce-scatter.9.cloned.1.call-start = ((), (), s32[]{:S(2)}) async-start(), calls=%async_computation.13 | async-start | bytes 10616832 | tf_op jit(solution)/shard_map/reduce_scatter | solution.py:261
  371.9 4.0 copy-start.42
  476.0 11.9 %copy-start.31 = (bf16[3072]{0:T(1024)(128)(2,1)S(1)}, bf16[3072]{0:T(1024)(128)(2,1)}, u32[]{:S(2)}) copy-start(bf16[3072]{0:T(1024)(128)(2,1)} %param.32) | copy-start | bytes 18436
  482.9 23.2 %all-to-all-start.1 = ((bf16[4,380,1,192]{3,0,2,1:T(4,128)(2,1)}), bf16[4,380,1,192]{3,0,2,1:T(4,128)(2,1)}, u32[]{:S(2)}, u32[]{:S(2)}) async-start(bf16[4,380,1,192]{3,0,2,1:T(4,128)(2,1)} %copy.184), calls=%async_computation.1 | async-start | bytes 1556480 | tf_op jit(solution)/shard_map/all_to_all | solution.py:125
  487.1 189.5 %all-reduce.8.cloned.1.call-start = ((), (), s32[]{:S(2)}) async-start(), calls=%async_computation.15 | async-start | bytes 184320 | tf_op jit(solution)/shard_map/psum | solution.py:265
  514.0 4.7 copy-start.3
  514.0 11.4 %copy-start.24 = (f32[380]{0:T(512)S(1)}, f32[380]{0:T(512)}, u32[]{:S(2)}) copy-start(f32[380]{0:T(512)} %copy-done.23) | copy-start | bytes 4564
  514.0 11.4 %copy-start.29 = (f32[380]{0:T(512)S(1)}, f32[380]{0:T(512)}, u32[]{:S(2)}) copy-start(f32[380]{0:T(512)} %copy-done.28) | copy-start | bytes 4564
  516.8 3.9 copy-start.47
  525.3 4.3 copy-start.37
  525.3 4.3 copy-start.2
  529.6 1.3 copy-start.8
  529.6 1.4 copy-start.10
  529.6 1.4 copy-start.39
  529.6 3.5 copy-start.35
  529.6 3.5 copy-start.46
  530.1 4.4 copy-start.33
  532.1 43.5 %copy-start.41 = (f32[768]{0:T(1024)S(1)}, f32[768]{0:T(1024)}, u32[]{:S(2)}) copy-start(f32[768]{0:T(1024)} %convert_element_type.184) | copy-start | bytes 9220
  532.1 43.6 %copy-start.48 = (f32[380]{0:T(512)S(1)}, f32[380]{0:T(512)}, u32[]{:S(2)}) copy-start(f32[380]{0:T(512)} %copy-done.47) | copy-start | bytes 4564
  534.4 275.2 %all-reduce.6.cloned.1.call-start = ((), (), s32[]{:S(2)}) async-start(), calls=%async_computation.10 | async-start | bytes 638976 | tf_op jit(solution)/shard_map/psum | solution.py:265
  537.3 410.5 %all-reduce.10.cloned.1.call-start = ((), (), s32[]{:S(2)}) async-start(), calls=%async_computation.16 | async-start | bytes 7077888 | tf_op jit(solution)/shard_map/psum | solution.py:264
  676.6 286.9 %copy-start.43 = (f32[3072]{0:T(1024)S(1)}, f32[3072]{0:T(1024)}, u32[]{:S(2)}) copy-start(f32[3072]{0:T(1024)} %get-tuple-element.212) | copy-start | bytes 36868
  947.8 14.8 %copy-start.19 = (f32[96,3072]{1,0:T(8,128)S(1)}, f32[96,3072]{1,0:T(8,128)}, u32[]{:S(2)}) copy-start(f32[96,3072]{1,0:T(8,128)} %get-tuple-element.211) | copy-start | bytes 3538948
  947.8 16.4 %copy-start.18 = (f32[384,768]{1,0:T(8,128)S(1)}, f32[384,768]{1,0:T(8,128)}, u32[]{:S(2)}) copy-start(f32[384,768]{1,0:T(8,128)} %get-tuple-element.213) | copy-start | bytes 3538948
  953.6 11.6 %copy-start.55 = (f32[768]{0:T(1024)S(1)}, f32[768]{0:T(1024)}, u32[]{:S(2)}) copy-start(f32[768]{0:T(1024)} %get-tuple-element.214) | copy-start | bytes 9220
  (6 other events, 5.0 us)
Sparse Core Ops, SparseCore 0:
  218.1 43.9 reduce-scatter.6
  350.7 64.5 reduce-scatter.4
  418.8 76.4 reduce-scatter.10
  498.6 76.9 reduce-scatter.8
Sparse Core Ops, SparseCore 1:
  534.5 142.1 all-reduce.7
  683.3 126.3 all-reduce.5
  812.2 135.6 all-reduce.9
where the time goes:
time: 980 us; the launch traced here: 974 us
  waiting for transfers between devices  423 us (43%)
  local copies, waits for them, and re-layouts  174 us (18%)
  blocking collectives  171 us (17%)
  matrix products  139 us (14%)
  other arithmetic  36.6 us (4%)
  between operations  16.5 us (2%)
  starting transfers between devices  13.9 us (1%)
    psum x2, waiting for transfers between devices, on_device(): lax.psum((freq_grad, time_grad, norm1_gain_grad, norm1_shift_grad, qv_bia...  207 us
    psum x1, waiting for transfers between devices, on_device(): shares = lax.psum((shares[0], shares[1], shares[2], shares[3]), 'seq')  138 us
    all_to_all x2, blocking collectives, forward(): lax.all_to_all(sending, 'seq', split_axis=3, concat_axis=1, tiled=True)  115 us
    all_to_all x1, blocking collectives, on_device(): lax.all_to_all(grad_qkv_heads, 'seq', split_axis=1, concat_axis=3, tiled=...  55.5 us
    unnamed x145, local copies, waits for them, and re-layouts  54.1 us
    reduce_scatter x1, waiting for transfers between devices, on_device(): lax.psum_scatter(matrices[2], 'clip', scatter_dimension=0, tiled=True)  37.4 us
    all_to_all x2, waiting for transfers between devices, forward(): lax.all_to_all(attended, 'seq', split_axis=1, concat_axis=2, tiled=True)  25.1 us
  transfers between devices with their start and end apart: 10, of which 7 were waited for; matrix products, arithmetic and copies ran while one was open for 22% of the time, Pallas kernels for 0%

commit v1 on v0

v1 whole, which is shorter than its diff:
```python
import functools

import jax
import jax.numpy as jnp
from jax import lax
from jax.experimental import pallas as pl
from jax.experimental.pallas import tpu as pltpu
from jax.sharding import PartitionSpec as P

F32, BF16 = jnp.float32, jnp.bfloat16
MESH = pl.DeviceIdType.MESH
HDIM = 64
FKEEP = 7
TKEEP = 54
SPLIT = 4
GROUP = 8
PAD = 16
TIMES = 112
SLOTS = 64
UNITS = 12
NT = (((1,), (1,)), ((), ()))
TN = (((0,), (0,)), ((), ()))
ERF_P = 0.3275911
ERF_C = (0.254829592, -0.284496736, 1.421413741, -1.453152027, 1.061405429)


def dot(a, b, dims=(((1,), (0,)), ((), ()))):
    return lax.dot_general(a, b, dims, preferred_element_type=F32)


def normal_cdf_pdf(h):
    bell = jnp.exp(-0.5 * h * h)
    t = 1.0 / (1.0 + (ERF_P * 2.0**-0.5) * jnp.abs(h))
    tail = ERF_C[4]
    for coefficient in ERF_C[3::-1]:
        tail = tail * t + coefficient
    tail = 0.5 * tail * t * bell
    return jnp.where(h >= 0, 1.0 - tail, tail), bell * 0.3989422804014327


def normalize(v):
    centered = v - jnp.mean(v, -1, keepdims=True)
    rstd = lax.rsqrt(jnp.mean(centered * centered, -1, keepdims=True) + 1e-06)
    return centered * rstd, rstd


def row(ref):
    return ref[...].astype(F32).reshape(1, -1)


def block_kernel(
    tokens, freq_index, time_index, freq_table, time_table,
    gain1, shift1, qkv_hbm, qv_bias, proj_hbm, proj_bias, gain2, shift2,
    fc1_hbm, fc1_bias, fc2_hbm, fc2_bias, cotangent,
    out_hbm, grad_hbm, shares_hbm, small_hbm,
    w_qkv, w_proj, w_fc1, w_fc2, tok_in, cot_in, stream_in, normed, qkv, probs, attended, mid,
    work, left, left_out, right, unit, got1, got2, end_in, mid_in, final, staged, staged_grad,
    tables, picks, pay, pay_in, pay_mid, pay_out,
    w_sem, tok_s, tok_r, cot_s, cot_r, out_s, out_r, grad_s, grad_r, left_s, left_r, right_s, right_r,
    one_s, one_r, two_s, two_r, end_s, end_r, mid_s, mid_r, fin_s, fin_r, share_s,
    pay_s, pay_r, payz_s, payz_r, payo_s, payo_r,
):
    width = stream_in.shape[1]
    rows = tok_in.shape[1]
    padded = stream_in.shape[0] // SPLIT
    many = stream_in.shape[0]
    shard = width // GROUP
    half = width // 2
    pairs = width // (2 * HDIM)
    heavy = 3 * width
    step = 256 if width % 256 == 0 else 128

    c, z = lax.axis_index("clip"), lax.axis_index("seq")
    low = c % GROUP
    core, x, y = low % 2, (low // 2) % 2, low // 4
    base = c - low

    def peer(bits):
        px = 1 - x if bits & 2 else x
        py = 1 - y if bits & 4 else y
        pc = 1 - core if bits & 1 else core
        return pc + 2 * px + 4 * py

    def at(bits):
        return (base + peer(bits), z)

    def along(d):
        return (c, (z + d) % SPLIT)

    is_end = (z == 0) | (z == SPLIT - 1)
    is_mid = (z == 1) | (z == 2)
    to_mid = (c, jnp.where(z == 0, 1, 2))
    to_end = (c, jnp.where(z == 1, 0, 3))
    to_other = (c, jnp.where(z == 1, 2, 1))

    def remote(src, dst, send, recv, device):
        return pltpu.make_async_remote_copy(
            src_ref=src, dst_ref=dst, send_sem=send, recv_sem=recv, device_id=device, device_id_type=MESH
        )

    weights = [
        pltpu.make_async_copy(src, dst, w_sem.at[i])
        for i, (src, dst) in enumerate(
            ((qkv_hbm, w_qkv), (proj_hbm, w_proj), (fc1_hbm, w_fc1), (fc2_hbm, w_fc2))
        )
    ]
    barrier = pltpu.get_barrier_semaphore()
    for d in range(1, SPLIT):
        pl.semaphore_signal(barrier, inc=1, device_id=along(d), device_id_type=MESH)
    for bits in range(1, GROUP):
        pl.semaphore_signal(barrier, inc=1, device_id=at(bits), device_id_type=MESH)
    own_tok = pltpu.make_async_copy(tokens.at[z], tok_in.at[z], tok_r.at[z])
    own_cot = pltpu.make_async_copy(cotangent.at[z], cot_in.at[z], cot_r.at[z])
    own_tok.start()
    own_cot.start()
    pl.semaphore_wait(barrier, SPLIT - 1 + GROUP - 1)

    def spread(src, dst, send, recv):
        return [
            remote(src.at[(z + d) % SPLIT], dst.at[z], send.at[d - 1], recv.at[z], along(d))
            for d in range(1, SPLIT)
        ]

    tok_out = spread(tokens, tok_in, tok_s, tok_r)
    cot_out = spread(cotangent, cot_in, cot_s, cot_r)
    for copy in tok_out:
        copy.start()
    for copy in weights:
        copy.start()

    def wait_block(src, dst, send, recv, k):
        @pl.when(z == k)
        def _():
            pltpu.make_async_copy(src.at[k], dst.at[k], recv.at[k]).wait()

        @pl.when(z != k)
        def _():
            remote(src.at[k], dst.at[k], send.at[0], recv.at[k], along(1)).wait_recv()

    lane = lax.broadcasted_iota(jnp.int32, (8, 128), 1)
    index = jnp.full((8, 128), -1, jnp.int32)
    for s in range(TKEEP):
        index = jnp.where(lane == s, time_index[z, s], index)
    for s in range(FKEEP):
        index = jnp.where(lane == SLOTS + s, freq_index[z, s] + TIMES, index)
    column = lax.broadcasted_iota(jnp.int32, (128, 128), 0)
    pick = jnp.where(column == index[:1], 1.0, 0.0)
    picks[...] = pick.astype(BF16)
    tables[...] = jnp.zeros_like(tables)
    tables[pl.ds(0, time_table.shape[0]), :] = time_table[...].astype(F32)
    tables[pl.ds(TIMES, freq_table.shape[0]), :] = freq_table[...].astype(F32)
    by_slot = dot(pick.T.astype(BF16), tables[...].astype(BF16)).astype(BF16)

    def slots_of(row_number, slot):
        block = sum((row_number >= padded * k).astype(jnp.int32) for k in range(1, SPLIT))
        inside = row_number - padded * block
        patch = row_number - (padded - rows) * block - 2
        frequency = sum((patch >= TKEEP * k).astype(jnp.int32) for k in range(1, FKEEP))
        time = patch - TKEEP * frequency
        hit = (slot == time) | (slot == SLOTS + frequency)
        return jnp.where(hit & (inside < rows) & (patch >= 0), 1.0, 0.0).astype(BF16)

    g1, s1 = row(gain1), row(shift1)
    for k in range(SPLIT):
        place = padded * k
        number = lax.broadcasted_iota(jnp.int32, (padded, 128), 0) + place
        slot = lax.broadcasted_iota(jnp.int32, (padded, 128), 1)
        position = dot(slots_of(number, slot), by_slot)
        wait_block(tokens, tok_in, tok_s, tok_r, k)
        stream_in[pl.ds(place, rows), :] = tok_in[k].astype(F32) + position[:rows]
        stream_in[pl.ds(place + rows, padded - rows), :] = jnp.zeros((padded - rows, width), F32)

        @pl.loop(0, padded // 32)
        def _(b):
            at_row = pl.ds(pl.multiple_of(place + b * 32, 32), 32)
            hat, _ = normalize(stream_in[at_row, :])
            normed[at_row, :] = (hat * g1 + s1).astype(BF16)

    for copy in cot_out:
        copy.start()

    def hand_left(i, q, turned):
        for side in range(2):

            @pl.when(core == side)
            def _():
                left[i, q, :, pl.ds(0, many)] = turned[side]
                left_out[i, q] = turned[1 - side]

    def left_copy(i):
        return remote(
            left_out.at[i], left.at[i, :, :, pl.ds(many, many)], left_s.at[i], left_r.at[i], at(1)
        )

    def hand_all(i, source):
        turned = source[...].T.reshape(4, 2, shard, many)
        for q in range(4):
            hand_left(i, q, turned[q])
        left_copy(i).start()

    def right_copy(g):
        return remote(
            right.at[g, pl.ds(0, many)], right.at[g, pl.ds(many, many)], right_s.at[g], right_r.at[g], at(1)
        )

    weights[0].wait()
    hand_all(6, normed)
    bias_q, bias_v = qv_bias[0:1, :].astype(F32), qv_bias[1:2, :].astype(F32)
    for t, (bias, scale) in enumerate(((bias_q, HDIM**-0.5), (None, 1.0), (bias_v, 1.0))):
        for n in range(0, width, step):
            part = dot(normed[...], w_qkv[:, pl.ds(t * width + n, step)])
            if bias is not None:
                part = part + bias[:, n : n + step]
            part = part.astype(BF16)
            if scale != 1.0:
                part = part * jnp.asarray(scale, BF16)
            qkv[:, pl.ds(t * width + n, step)] = part

    key_number = lax.broadcasted_iota(jnp.int32, (8, many), 1)
    key_block = sum((key_number >= padded * k).astype(jnp.int32) for k in range(1, SPLIT))
    key_mask = jnp.where(key_number - padded * key_block < rows, 0.0, -1e30)[:1]
    head_lane = lax.broadcasted_iota(jnp.int32, (8, 2 * HDIM), 1)
    one_head = [
        jnp.where(head_lane < HDIM, 1.0, 0.0)[:1].astype(BF16),
        jnp.where(head_lane < HDIM, 0.0, 1.0)[:1].astype(BF16),
    ]

    def lanes(t, p):
        return pl.ds(pl.multiple_of(t * width + p * (2 * HDIM), 2 * HDIM), 2 * HDIM)

    @pl.loop(0, pairs)
    def _(p):
        query, key, value = (qkv[:, lanes(t, p)] for t in range(3))
        total = None
        for h in range(2):
            scores = dot(query * one_head[h], key, NT) + key_mask
            weight = jnp.exp(scores - jnp.max(scores, -1, keepdims=True))
            weight = (weight * (1.0 / jnp.sum(weight, -1, keepdims=True))).astype(BF16)
            probs[2 * p + h] = weight
            part = dot(weight, value * one_head[h])
            total = part if total is None else total + part
        attended[:, lanes(0, p)] = total.astype(BF16)

    weights[1].wait()
    hand_all(5, attended)
    bias = row(proj_bias)
    for n in range(0, width, step):
        mid[:, pl.ds(n, step)] = (
            stream_in[:, pl.ds(n, step)]
            + dot(attended[...], w_proj[:, pl.ds(n, step)])
            + bias[:, n : n + step]
        )
    g2, s2 = row(gain2), row(shift2)

    @pl.loop(0, many // 32)
    def _(b):
        at_row = pl.ds(pl.multiple_of(b * 32, 32), 32)
        hat, _ = normalize(mid[at_row, :])
        normed[at_row, :] = (hat * g2 + s2).astype(BF16)

    weights[2].wait()
    hand_all(4, normed)
    for q in range(4):
        for n in range(0, width, step):
            place = q * width + n
            work[:, pl.ds(n, step)] = (
                dot(normed[...], w_fc1[:, pl.ds(place, step)])
                + fc1_bias[pl.ds(place, step)].astype(F32).reshape(1, step)
            )

        @pl.loop(0, many // 32)
        def _(b):
            at_row = pl.ds(pl.multiple_of(b * 32, 32), 32)
            hidden = work[at_row, :]
            cdf, pdf = normal_cdf_pdf(hidden)
            unit[8 + q, at_row, :] = (hidden * cdf).astype(BF16)
            right[1 + q, at_row, :] = (cdf + hidden * pdf).astype(BF16)

        turned = unit[8 + q].T.reshape(2, 4, shard, many)
        for u in range(4):
            hand_left(u, q, turned[:, u])

    for u in range(4):
        left_copy(u).start()

    for k in range(SPLIT):
        place = padded * k
        wait_block(cotangent, cot_in, cot_s, cot_r, k)
        work[pl.ds(place, rows), :] = cot_in[k].astype(F32)
        work[pl.ds(place + rows, padded - rows), :] = jnp.zeros((padded - rows, width), F32)
    right[0, pl.ds(0, many), :] = work[...].astype(BF16)
    right_copy(0).start()

    def column_sums(ref_value):
        return jnp.sum(ref_value.astype(F32), 0, keepdims=True)

    pay[pl.ds(99 + 7, 1), :] = column_sums(work[...])

    A, B = pl.ds(0, half), pl.ds(half, half)

    def grid_of(i):
        return unit.at[i].reshape(2, 2, shard, width)

    def one_copies(i):
        u = grid_of(i)
        return (
            remote(u.at[:, 1 - x, :, A], got1.at[i, 0], one_s.at[i, 0], one_r.at[i, 0], at(2)),
            remote(u.at[1 - y, :, :, B], got1.at[i, 1], one_s.at[i, 1], one_r.at[i, 1], at(4)),
        )

    def two_copies(i):
        u = grid_of(i)
        return (
            remote(u.at[1 - y, x, :, A], got2.at[i, 0], two_s.at[i, 0], two_r.at[i, 0], at(4)),
            remote(u.at[y, 1 - x, :, B], got2.at[i, 1], two_s.at[i, 1], two_r.at[i, 1], at(2)),
        )

    def end_copy(i):
        return remote(grid_of(i).at[y, x], end_in.at[i], end_s.at[i], end_r.at[i], to_mid)

    own_part = jnp.where(z == 2, 1, 0)
    oth_part = 1 - own_part
    own_cols = pl.ds(pl.multiple_of(own_part * half, 128), half)
    oth_cols = pl.ds(pl.multiple_of(oth_part * half, 128), half)

    def mid_copy(i):
        return remote(grid_of(i).at[y, x, :, oth_cols], mid_in.at[i], mid_s.at[i], mid_r.at[i], to_other)

    def fin_copy(i, part, cols, which, device):
        return remote(final.at[i, :, cols], final.at[i, :, cols], fin_s.at[i, which], fin_r.at[i, part], device)

    def share_copy(i):
        return pltpu.make_async_copy(final.at[i], shares_hbm.at[i], share_s.at[i])

    def product(i, l, g, first_left, first_right):
        if first_left:
            left_copy(l).wait_recv()
        if first_right:
            right_copy(g).wait_recv()
        for n in range(0, width, step):
            part = dot(left[l].reshape(4 * shard, 2 * many), right[g, :, pl.ds(n, step)])
            unit[i, :, pl.ds(n, step)] = part.astype(BF16)
        for copy in one_copies(i):
            copy.start()

    def tick1(i):
        u = grid_of(i)
        first, second = one_copies(i)
        first.wait_recv()
        second.wait_recv()
        u[1 - y, x, :, A] = (u[1 - y, x, :, A].astype(F32) + got1[i, 0, 1 - y].astype(F32)).astype(BF16)
        u[y, 1 - x, :, B] = (u[y, 1 - x, :, B].astype(F32) + got1[i, 1, 1 - x].astype(F32)).astype(BF16)
        for copy in two_copies(i):
            copy.start()

    def tick2(i):
        for copy in two_copies(i):
            copy.wait_recv()

        @pl.when(is_end)
        def _():
            u = grid_of(i)
            u[y, x, :, A] = (
                u[y, x, :, A].astype(F32) + got1[i, 0, y].astype(F32) + got2[i, 0].astype(F32)
            ).astype(BF16)
            u[y, x, :, B] = (
                u[y, x, :, B].astype(F32) + got1[i, 1, x].astype(F32) + got2[i, 1].astype(F32)
            ).astype(BF16)
            end_copy(i).start()

    def sum_of(i, part, cols):
        near = jnp.where(part == 0, y, x)
        return (
            grid_of(i)[y, x, :, cols].astype(F32)
            + got1[i, part, near].astype(F32)
            + got2[i, part].astype(F32)
            + end_in[i, :, cols].astype(F32)
        )

    def tick3(i):
        @pl.when(is_mid)
        def _():
            end_copy(i).wait_recv()
            grid_of(i)[y, x, :, oth_cols] = sum_of(i, oth_part, oth_cols).astype(BF16)
            mid_copy(i).start()

    def tick4(i):
        @pl.when(is_mid)
        def _():
            mid_copy(i).wait_recv()
            final[i, :, own_cols] = (sum_of(i, own_part, own_cols) + mid_in[i].astype(F32)).astype(BF16)
            fin_copy(i, own_part, own_cols, 0, to_other).start()
            fin_copy(i, own_part, own_cols, 1, to_end).start()

    def tick5(i):
        @pl.when(is_mid)
        def _():
            fin_copy(i, oth_part, oth_cols, 2, to_end).wait_recv()
            fin_copy(i, oth_part, oth_cols, 2, to_end).start()

        @pl.when(is_end)
        def _():
            fin_copy(i, 0, A, 0, to_mid).wait_recv()
            fin_copy(i, 1, B, 0, to_mid).wait_recv()

        share_copy(i).start()

    ticks = (tick1, tick2, tick3, tick4, tick5)

    def advance(n):
        for k in range(len(ticks) - 1, -1, -1):
            if 0 <= n - k < UNITS:
                ticks[k](n - k)

    for i in range(4):
        product(i, i, 0, True, i == 0)

    weights[3].wait()
    bias = row(fc2_bias)
    for n in range(0, width, step):
        part = mid[:, pl.ds(n, step)] + bias[:, n : n + step]
        for q in range(4):
            part = part + dot(unit[8 + q], w_fc2[pl.ds(q * width, width), pl.ds(n, step)])
        for k in range(SPLIT):
            staged[k, :, pl.ds(n, step)] = part[padded * k : padded * k + rows].astype(BF16)

    def give(src, dst, send, recv):
        own = pltpu.make_async_copy(src.at[z], dst.at[z], recv.at[z])
        return [own] + [
            remote(src.at[(z + d) % SPLIT], dst.at[z], send.at[d - 1], recv.at[z], along(d))
            for d in range(1, SPLIT)
        ]

    out_copies = give(staged, out_hbm, out_s, out_r)
    for copy in out_copies:
        copy.start()
    advance(0)

    def grad_hidden(q):
        for n in range(0, width, step):
            part = dot(right[0, pl.ds(0, many), :], w_fc2[pl.ds(q * width + n, step), :], NT)
            part = (part * right[1 + q, pl.ds(0, many), pl.ds(n, step)].astype(F32)).astype(BF16)
            right[1 + q, pl.ds(0, many), pl.ds(n, step)] = part
            pay[pl.ds(99 + 8 + q, 1), pl.ds(n, step)] = column_sums(part)
        right_copy(1 + q).start()

    grad_hidden(0)
    grad_hidden(1)
    product(4, 4, 1, True, True)
    product(5, 4, 2, False, True)
    advance(1)
    grad_hidden(2)
    grad_hidden(3)
    product(6, 4, 3, False, True)
    product(7, 4, 4, False, True)
    advance(2)

    for n in range(0, width, step):
        part = None
        for q in range(4):
            term = dot(right[1 + q, pl.ds(0, many), :], w_fc1[pl.ds(n, step), pl.ds(q * width, width)], NT)
            part = term if part is None else part + term
        work[:, pl.ds(n, step)] = part

    def norm_back(grad, value, gain):
        hat, rstd = normalize(value)
        g = grad * gain
        back = rstd * (g - jnp.mean(g, -1, keepdims=True) - hat * jnp.mean(g * hat, -1, keepdims=True))
        return back, hat

    zero = jnp.zeros((1, width), F32)

    def back_second(b, sums):
        at_row = pl.ds(pl.multiple_of(b * 32, 32), 32)
        grad = work[at_row, :]
        back, hat = norm_back(grad, mid[at_row, :], g2)
        back = back + right[0, at_row, :].astype(F32)
        mid[at_row, :] = back
        branch = back.astype(BF16)
        right[5, at_row, :] = branch
        return (
            sums[0] + column_sums(grad * hat),
            sums[1] + column_sums(grad),
            sums[2] + column_sums(branch),
        )

    sums = lax.fori_loop(0, many // 32, back_second, (zero, zero, zero))
    pay[pl.ds(99 + 5, 1), :] = sums[0]
    pay[pl.ds(99 + 6, 1), :] = sums[1]
    pay[pl.ds(99 + 4, 1), :] = sums[2]
    right_copy(5).start()
    for n in range(0, width, step):
        normed[:, pl.ds(n, step)] = dot(
            right[5, pl.ds(0, many), :], w_proj[pl.ds(n, step), :], NT
        ).astype(BF16)
    product(8, 5, 5, True, True)
    advance(3)

    def attend_back(p):
        query, key, value = (qkv[:, lanes(t, p)] for t in range(3))
        grad_out = normed[:, lanes(0, p)]
        grads = None
        for h in range(2):
            weight_low = probs[2 * p + h]
            weight = weight_low.astype(F32)
            grad_probs = dot(grad_out * one_head[h], value, NT) * weight
            inner = jnp.sum(grad_probs, -1, keepdims=True)
            grad_scores = (grad_probs - weight * inner).astype(BF16)
            terms = (
                dot(grad_scores, key * one_head[h]),
                dot(grad_scores, query * one_head[h], TN),
                dot(weight_low, grad_out * one_head[h], TN),
            )
            grads = terms if grads is None else tuple(a + b for a, b in zip(grads, terms, strict=True))
        for t, (grad, scale) in enumerate(zip(grads, (HDIM**-0.5, 1.0, 1.0), strict=True)):
            low_grad = (grad * scale).astype(BF16)
            right[6 + t, pl.ds(0, many), lanes(0, p)] = low_grad
            if t != 1:
                pay[pl.ds(99 + 2 + t // 2, 1), lanes(0, p)] = column_sums(low_grad)

    parts = 3
    for s in range(parts):
        @pl.loop(s * pairs // parts, (s + 1) * pairs // parts)
        def _(p):
            attend_back(p)

        if s < parts - 1:
            advance(4 + s)
    for t in range(3):
        right_copy(6 + t).start()
    for t in range(3):
        product(9 + t, 6, 6 + t, t == 0, True)
    advance(6)

    for n in range(0, width, step):
        part = None
        for t in range(3):
            term = dot(right[6 + t, pl.ds(0, many), :], w_qkv[pl.ds(n, step), pl.ds(t * width, width)], NT)
            part = term if part is None else part + term
        work[:, pl.ds(n, step)] = part

    def back_first(b, sums):
        at_row = pl.ds(pl.multiple_of(b * 32, 32), 32)
        grad = work[at_row, :]
        back, hat = norm_back(grad, stream_in[at_row, :], g1)
        mid[at_row, :] = mid[at_row, :] + back
        return sums[0] + column_sums(grad * hat), sums[1] + column_sums(grad)

    sums = lax.fori_loop(0, many // 32, back_first, (zero, zero))
    pay[pl.ds(99, 1), :] = sums[0]
    pay[pl.ds(100, 1), :] = sums[1]
    for k in range(SPLIT):
        staged_grad[k] = mid[pl.ds(padded * k, padded), :][:rows].astype(BF16)
    grad_copies = give(staged_grad, grad_hbm, grad_s, grad_r)
    for copy in grad_copies:
        copy.start()

    def halves(v):
        high = v.astype(BF16)
        return high, (v - high.astype(F32)).astype(BF16)

    number = lax.broadcasted_iota(jnp.int32, (128, many), 1)
    slot = lax.broadcasted_iota(jnp.int32, (128, many), 0)
    slots = slots_of(number, slot)
    for n in range(0, width, step):
        by = sum(dot(slots, v) for v in halves(mid[:, pl.ds(n, step)]))
        table_grad = sum(dot(picks[...], v) for v in halves(by))
        pay[pl.ds(0, 99), pl.ds(n, step)] = table_grad[:99]
        pay[pl.ds(TIMES, 16), pl.ds(n, step)] = table_grad[TIMES:]
    pay[pl.ds(111, 1), :] = zero

    def pay_copy(bits):
        return remote(pay.at[pl.ds(16 * peer(bits), 16)], pay_in.at[low], pay_s.at[bits - 1], pay_r.at[low], at(bits))

    def pay_wait(bits):
        remote(
            pay.at[pl.ds(0, 16)], pay_in.at[peer(bits)], pay_s.at[bits - 1], pay_r.at[peer(bits)], at(bits)
        ).wait_recv()

    def payz_copy(d):
        return remote(pay_mid.at[z], pay_mid.at[z], payz_s.at[d - 1], payz_r.at[z], along(d))

    def payo_copy(bits):
        return remote(pay_out.at[low], pay_out.at[low], payo_s.at[bits - 1], payo_r.at[low], at(bits))

    for bits in range(1, GROUP):
        pay_copy(bits).start()
    advance(7)
    for bits in range(1, GROUP):
        pay_wait(bits)
    pay_in[low] = pay[pl.ds(pl.multiple_of(16 * low, 16), 16), :]
    pay_mid[z] = sum(pay_in[s] for s in range(GROUP))
    for d in range(1, SPLIT):
        payz_copy(d).start()
    advance(8)
    for d in range(1, SPLIT):
        k = (z + d) % SPLIT
        remote(pay_mid.at[k], pay_mid.at[k], payz_s.at[d - 1], payz_r.at[k], along(d)).wait_recv()
    pay_out[low] = sum(pay_mid[s] for s in range(SPLIT))
    for bits in range(1, GROUP):
        payo_copy(bits).start()
    for n in range(9, UNITS + len(ticks) - 1):
        advance(n)
    for bits in range(1, GROUP):
        remote(
            pay_out.at[low], pay_out.at[peer(bits)], payo_s.at[bits - 1], payo_r.at[peer(bits)], at(bits)
        ).wait_recv()
    last = pltpu.make_async_copy(pay_out, small_hbm, w_sem.at[0])
    last.start()

    for copies in (tok_out, cot_out, out_copies[1:], grad_copies[1:]):
        for copy in copies:
            copy.wait_send()
    for k in range(SPLIT):
        wait_block(staged, out_hbm, out_s, out_r, k)
        wait_block(staged_grad, grad_hbm, grad_s, grad_r, k)
    for i in range(left.shape[0]):
        left_copy(i).wait_send()
    for g in range(right.shape[0]):
        right_copy(g).wait_send()

    @pl.loop(0, UNITS)
    def _(i):
        for copy in (*one_copies(i), *two_copies(i)):
            copy.wait_send()

        @pl.when(is_end)
        def _():
            end_copy(i).wait_send()

        @pl.when(is_mid)
        def _():
            mid_copy(i).wait_send()
            fin_copy(i, own_part, own_cols, 0, to_other).wait_send()
            fin_copy(i, own_part, own_cols, 1, to_end).wait_send()
            fin_copy(i, oth_part, oth_cols, 2, to_end).wait_send()

        share_copy(i).wait()

    for bits in range(1, GROUP):
        pay_copy(bits).wait_send()
        payo_copy(bits).wait_send()
    for d in range(1, SPLIT):
        payz_copy(d).wait_send()
    last.wait()


def on_device(
    tokens, freq_index, time_index, freq_table, time_table,
    norm1_gain, norm1_shift, qkv_weight, qv_bias, proj_weight, proj_bias, norm2_gain, norm2_shift,
    fc1_weight, fc1_bias, fc2_weight, fc2_bias, cotangent,
):
    clips, rows, width = tokens.shape
    groups = lax.axis_size("seq")
    clip_devices = lax.axis_size("clip")
    assert clips == SPLIT and groups == SPLIT and clip_devices % GROUP == 0
    hidden_width = fc1_weight.shape[1]
    assert hidden_width == 4 * width
    padded = -(-rows // 32) * 32
    many = SPLIT * padded
    shard = width // GROUP
    half = width // 2
    heads = width // HDIM

    vmem = pl.BlockSpec(memory_space=pltpu.VMEM)
    smem = pl.BlockSpec(memory_space=pltpu.SMEM)
    anywhere = pl.BlockSpec(memory_space=pl.ANY)
    dma = pltpu.SemaphoreType.DMA
    blocks = (SPLIT, rows, width)
    out, grad, shares, small = pl.pallas_call(
        block_kernel,
        out_shape=(
            jax.ShapeDtypeStruct(blocks, BF16),
            jax.ShapeDtypeStruct(blocks, BF16),
            jax.ShapeDtypeStruct((UNITS, shard, width), BF16),
            jax.ShapeDtypeStruct((GROUP, 16, width), F32),
        ),
        in_specs=[
            anywhere, smem, smem, vmem, vmem, vmem, vmem, anywhere, vmem, anywhere, vmem, vmem, vmem,
            anywhere, vmem, anywhere, vmem, anywhere,
        ],
        out_specs=(anywhere,) * 4,
        scratch_shapes=[
            pltpu.VMEM((width, 3 * width), BF16),
            pltpu.VMEM((width, width), BF16),
            pltpu.VMEM((width, hidden_width), BF16),
            pltpu.VMEM((hidden_width, width), BF16),
            pltpu.VMEM(blocks, BF16),
            pltpu.VMEM(blocks, BF16),
            pltpu.VMEM((many, width), F32),
            pltpu.VMEM((many, width), BF16),
            pltpu.VMEM((many, 3 * width), BF16),
            pltpu.VMEM((heads, many, many), BF16),
            pltpu.VMEM((many, width), BF16),
            pltpu.VMEM((many, width), F32),
            pltpu.VMEM((many, width), F32),
            pltpu.VMEM((7, 4, shard, 2 * many), BF16),
            pltpu.VMEM((7, 4, shard, many), BF16),
            pltpu.VMEM((9, 2 * many, width), BF16),
            pltpu.VMEM((UNITS, 4 * shard, width), BF16),
            pltpu.VMEM((UNITS, 2, 2, shard, half), BF16),
            pltpu.VMEM((UNITS, 2, shard, half), BF16),
            pltpu.VMEM((UNITS, shard, width), BF16),
            pltpu.VMEM((UNITS, shard, half), BF16),
            pltpu.VMEM((UNITS, shard, width), BF16),
            pltpu.VMEM(blocks, BF16),
            pltpu.VMEM(blocks, BF16),
            pltpu.VMEM((128, width), F32),
            pltpu.VMEM((128, 128), BF16),
            pltpu.VMEM((128, width), F32),
            pltpu.VMEM((GROUP, 16, width), F32),
            pltpu.VMEM((SPLIT, 16, width), F32),
            pltpu.VMEM((GROUP, 16, width), F32),
            dma((4,)),
            dma((3,)), dma((4,)), dma((3,)), dma((4,)), dma((3,)), dma((4,)), dma((3,)), dma((4,)),
            dma((7,)), dma((7,)), dma((9,)), dma((9,)),
            dma((UNITS, 2)), dma((UNITS, 2)), dma((UNITS, 2)), dma((UNITS, 2)),
            dma((UNITS,)), dma((UNITS,)), dma((UNITS,)), dma((UNITS,)),
            dma((UNITS, 3)), dma((UNITS, 2)), dma((UNITS,)),
            dma((7,)), dma((8,)), dma((3,)), dma((4,)), dma((7,)), dma((8,)),
        ],
        compiler_params=pltpu.CompilerParams(
            collective_id=1, has_side_effects=True, vmem_limit_bytes=63 * 2**20
        ),
    )(
        tokens, freq_index, time_index, freq_table, time_table,
        norm1_gain, norm1_shift, qkv_weight, qv_bias, proj_weight, proj_bias, norm2_gain, norm2_shift,
        fc1_weight, fc1_bias, fc2_weight, fc2_bias, cotangent,
    )
    shares = shares.astype(F32)
    small = small.reshape(GROUP * 16, width)
    if clip_devices > GROUP:
        count = clip_devices // GROUP
        same = [[h * GROUP + b for h in range(count)] for b in range(GROUP)]
        small = lax.psum(small, "clip", axis_index_groups=same)
        fc2 = shares[:4].reshape(4 * shard, width)
        rest = shares[4:].transpose(1, 0, 2).reshape(shard, 8 * width)
        summed = [
            lax.psum_scatter(v, "clip", scatter_dimension=0, axis_index_groups=same, tiled=True)
            for v in (fc2, rest)
        ]
        moves = [(h * GROUP + b, b * count + h) for h in range(count) for b in range(GROUP)]
        fc2, rest = (lax.ppermute(v, "clip", moves) for v in summed)
    else:
        fc2 = shares[:4].reshape(4 * shard, width)
        rest = shares[4:].transpose(1, 0, 2).reshape(shard, 8 * width)
    fc1, proj, qkv = rest[:, : 4 * width], rest[:, 4 * width : 5 * width], rest[:, 5 * width :]
    return (
        out,
        grad,
        small[TIMES : TIMES + freq_table.shape[0]],
        small[: time_table.shape[0]],
        small[99],
        small[100],
        qkv,
        small[101:103],
        proj,
        small[103],
        small[104],
        small[105],
        fc1,
        small[107:111].reshape(-1),
        fc2,
        small[106],
    )


def solution(mesh):
    rows_split, clip_split = P("clip", "seq", None), P("clip", None)
    in_specs = (rows_split, clip_split, clip_split) + (P(),) * 14 + (rows_split,)
    out_specs = (
        rows_split, rows_split, P(), P(), P(), P(), clip_split, P(), clip_split, P(), P(), P(), clip_split,
        P(), clip_split, P(),
    )
    return jax.shard_map(on_device, mesh=mesh, in_specs=in_specs, out_specs=out_specs, check_vma=False)
```

time: 980 us -> 184 us (0.19)
  waiting for transfers between devices: 423 us -> 0 us
  blocking collectives: 171 us -> 0 us
  Pallas kernels: 0 us -> 162 us
  local copies, waits for them, and re-layouts: 174 us -> 20.3 us
  matrix products: 139 us -> 0 us
  other arithmetic: 36.6 us -> 0.32 us
  between operations: 16.5 us -> 0.69 us
  starting transfers between devices: 13.9 us -> 0 us
    psum x3 -> x0, waiting for transfers between devices: 345 us -> none  [the longest x2 207 us: on_device(): lax.psum((freq_grad, time_grad, norm1_gain_grad, norm1_shift_grad, qv_bia...]
    all_to_all x3 -> x0, blocking collectives: 171 us -> none  [the longest x2 115 us: forward(): lax.all_to_all(sending, 'seq', split_axis=3, concat_axis=1, tiled=True)]
    pallas_call x0 -> x1, Pallas kernels: none -> 162 us  [on_device(): pl.pallas_call(block_kernel, out_shape=(jax.ShapeDtypeStruct(blocks, BF16...]
    dot_general x24 -> x0, matrix products: 125 us -> none  [the longest x1 18.5 us: forward(): jnp.dot(activated, fc2_weight, preferred_element_type=jnp.float32)]
    reshape x17 -> x2, local copies, waits for them, and re-layouts: 64.1 us -> 0.82 us  [the longest x1 0.61 us: on_device(): small[107:111].reshape(-1)]
    unnamed x145 -> x7, local copies, waits for them, and re-layouts: 54.1 us -> 8.82 us
    all_to_all x3 -> x0, waiting for transfers between devices: 40.8 us -> none  [the longest x2 25.1 us: forward(): lax.all_to_all(attended, 'seq', split_axis=1, concat_axis=2, tiled=True)]
    reduce_scatter x4 -> x0, waiting for transfers between devices: 37.4 us -> none  [the longest x1 37.4 us: on_device(): lax.psum_scatter(matrices[2], 'clip', scatter_dimension=0, tiled=True)]
  transfers between devices with their start and end apart: 10 -> 0, of which waited for: 7 -> 0; matrix products, arithmetic and copies ran while one was open for 22% -> 0% of each run, Pallas kernels for 0% -> 0%
where the time goes in v1:
time: 184 us; the launch traced here: 183 us
  Pallas kernels  162 us (88%)
  local copies, waits for them, and re-layouts  20.3 us (11%)
    pallas_call x1, Pallas kernels, on_device(): pl.pallas_call(block_kernel, out_shape=(jax.ShapeDtypeStruct(blocks, BF16...  162 us
    unnamed x7, local copies, waits for them, and re-layouts  8.82 us

profile of v1, /device:TPU:0, one launch (start us, length us, event | category | flops | bytes accessed | tf_op | source)
XLA Modules:
  0.0 183.2 jit_solution(17738428955839244368)
XLA Ops:
  0.6 1.9 %copy.38.tokens = bf16[4,95,768]{2,1,0:T(8,128)(2,1)} copy(bf16[4,95,768]{2,0,1:T(4,128)(2,1)} %param.18) | data formatting | bytes 1167360 | tf_op args[0]
  2.6 1.9 %copy.39.cotangent = bf16[4,95,768]{2,1,0:T(8,128)(2,1)} copy(bf16[4,95,768]{2,0,1:T(4,128)(2,1)} %param.35) | data formatting | bytes 1167360 | tf_op args[17]
  4.5 161.9 %shard_map.297 = (bf16[4,95,768]{2,1,0:T(8,128)(2,1)}, bf16[4,95,768]{2,1,0:T(8,128)(2,1)}, bf16[12,96,768]{2,1,0:T(8,128)(2,1)}, f32[8,16,768]{2,1,0:T(8,128)}) custom-call(bf16[4,95,768]{2,1,0:T(8,128)(2,1)} %copy.38.tokens, s32[4,7]{1,0:T(4,128)} %freq_index.1, s32[4,54]{1,0:T(4,128)} %time_index.1, bf16[12,768]{1,0:T(8,128)(2,1)} %freq_table.1, ...), custom_call_target="tpu_custom_call" | custom-call | tf_op jit(solution)/shard_map/pallas_call | solution.py:670
  166.5 0.0 copy-start
  166.5 2.5 %copy.41 = bf16[4,95,768]{2,0,1:T(4,128)(2,1)} copy(bf16[4,95,768]{2,1,0:T(8,128)(2,1)} %get-tuple-element.40) | data formatting | bytes 1167360
  168.9 1.3 slice.66
  170.3 0.7 slice.72
  171.0 0.6 reshape.46
  171.6 1.5 slice_reduce_fusion
  173.2 1.4 slice.60
  174.6 1.7 slice.61
  176.3 2.3 %copy.42 = bf16[4,95,768]{2,0,1:T(4,128)(2,1)} copy(bf16[4,95,768]{2,1,0:T(8,128)(2,1)} %get-tuple-element.41) | data formatting | bytes 1167360
  178.6 0.0 copy-done
  178.6 1.1 slice.73
  179.7 0.3 convert_element_type.3
  180.1 0.2 slice_bitcast_fusion
  180.2 0.2 copy.43
  180.4 0.7 slice.67
  181.2 1.0 slice.65
  182.1 1.1 slice.71
Async XLA Ops:
  166.5 12.2 %copy-start = (bf16[12,96,768]{2,1,0:T(8,128)(2,1)S(1)}, bf16[12,96,768]{2,1,0:T(8,128)(2,1)}, u32[]{:S(2)}) copy-start(bf16[12,96,768]{2,1,0:T(8,128)(2,1)} %get-tuple-element.23) | copy-start | bytes 5308420

commit v2 on v1

--- a/solution.py
+++ b/solution.py
@@ -17,7 +17,17 @@
 PAD = 16
 TIMES = 112
 SLOTS = 64
+BLOCK = 96
 UNITS = 12
+ORDER = (
+    "t0_0", "t0_1", "gh0", "gh1", "t0_2", "gh2", "gh3", "out", "sec", "t1_0", "t0_3", "sen", "t1_1", "t0_4", "att",
+    "ab0", "t2_0", "ab1", "t1_2", "t0_5", "ab2", "fir", "t2_1", "t1_3", "fin", "t0_6", "t3_0", "t2_2", "tab", "t1_4",
+    "t0_7", "pay2", "t3_1", "t2_3", "t1_5", "t0_8", "t4_0", "pay3", "t3_2", "t2_4", "t1_6", "t0_9", "t4_1", "t5_0",
+    "t3_3", "t2_5", "t1_7", "t0_10", "t4_2", "t5_1", "t3_4", "t2_6", "t1_8", "t0_11", "t4_3", "t5_2", "t3_5", "t2_7",
+    "t1_9", "t4_4", "t5_3", "t3_6", "t2_8", "t1_10", "t4_5", "t5_4", "t3_7", "t2_9", "t1_11", "t4_6", "t5_5", "t3_8",
+    "t2_10", "t4_7", "t5_6", "t3_9", "t2_11", "t4_8", "t5_7", "t3_10", "t4_9", "t5_8", "t3_11", "t4_10", "t5_9",
+    "t4_11", "t5_10", "t5_11",
+)
 NT = (((1,), (1,)), ((), ()))
 TN = (((0,), (0,)), ((), ()))
 ERF_P = 0.3275911
@@ -49,14 +59,15 @@
 
 
 def block_kernel(
-    tokens, freq_index, time_index, freq_table, time_table,
-    gain1, shift1, qkv_hbm, qv_bias, proj_hbm, proj_bias, gain2, shift2,
-    fc1_hbm, fc1_bias, fc2_hbm, fc2_bias, cotangent,
+    tokens, freq_index_hbm, time_index_hbm, freq_table_hbm, time_table_hbm,
+    gain1_hbm, shift1_hbm, qkv_hbm, qv_bias_hbm, proj_hbm, proj_bias_hbm, gain2_hbm, shift2_hbm,
+    fc1_hbm, fc1_bias_hbm, fc2_hbm, fc2_bias_hbm, cotangent,
     out_hbm, grad_hbm, shares_hbm, small_hbm,
-    w_qkv, w_proj, w_fc1, w_fc2, tok_in, cot_in, stream_in, normed, qkv, probs, attended, mid,
+    freq_index, time_index, freq_table, time_table, gain1, shift1, qv_bias, proj_bias, gain2, shift2, fc1_bias, fc2_bias,
+    raw, wide, w_qkv, w_proj, w_fc1, w_fc2, tok_in, cot_in, wide_cot, stream_in, normed, qkv, probs, attended, mid,
     work, left, left_out, right, unit, got1, got2, end_in, mid_in, final, staged, staged_grad,
-    tables, picks, pay, pay_in, pay_mid, pay_out,
-    w_sem, tok_s, tok_r, cot_s, cot_r, out_s, out_r, grad_s, grad_r, left_s, left_r, right_s, right_r,
+    picks, pay, pay_low, pay_in, pay_mid, pay_out,
+    v_sem, raw_sem, w_sem, tok_s, tok_r, cot_s, cot_r, out_s, out_r, grad_s, grad_r, left_s, left_r, right_s, right_r,
     one_s, one_r, two_s, two_r, end_s, end_r, mid_s, mid_r, fin_s, fin_r, share_s,
     pay_s, pay_r, payz_s, payz_r, payo_s, payo_r,
 ):
@@ -98,22 +109,33 @@
             src_ref=src, dst_ref=dst, send_sem=send, recv_sem=recv, device_id=device, device_id_type=MESH
         )
 
+    small = [
+        pltpu.make_async_copy(src, dst, v_sem.at[i])
+        for i, (src, dst) in enumerate(
+            (
+                (freq_index_hbm, freq_index), (time_index_hbm, time_index),
+                (freq_table_hbm, freq_table), (time_table_hbm, time_table),
+                (gain1_hbm, gain1), (shift1_hbm, shift1), (qv_bias_hbm, qv_bias), (proj_bias_hbm, proj_bias),
+                (gain2_hbm, gain2), (shift2_hbm, shift2), (fc1_bias_hbm, fc1_bias), (fc2_bias_hbm, fc2_bias),
+            )
+        )
+    ]
     weights = [
         pltpu.make_async_copy(src, dst, w_sem.at[i])
         for i, (src, dst) in enumerate(
             ((qkv_hbm, w_qkv), (proj_hbm, w_proj), (fc1_hbm, w_fc1), (fc2_hbm, w_fc2))
         )
     ]
+    raw_tok = pltpu.make_async_copy(tokens, raw, raw_sem.at[0])
+    raw_cot = pltpu.make_async_copy(cotangent, raw, raw_sem.at[1])
+    raw_tok.start()
     barrier = pltpu.get_barrier_semaphore()
     for d in range(1, SPLIT):
         pl.semaphore_signal(barrier, inc=1, device_id=along(d), device_id_type=MESH)
     for bits in range(1, GROUP):
         pl.semaphore_signal(barrier, inc=1, device_id=at(bits), device_id_type=MESH)
-    own_tok = pltpu.make_async_copy(tokens.at[z], tok_in.at[z], tok_r.at[z])
-    own_cot = pltpu.make_async_copy(cotangent.at[z], cot_in.at[z], cot_r.at[z])
-    own_tok.start()
-    own_cot.start()
-    pl.semaphore_wait(barrier, SPLIT - 1 + GROUP - 1)
+    for copy in small:
+        copy.start()
 
     def spread(src, dst, send, recv):
         return [
@@ -121,12 +143,30 @@
             for d in range(1, SPLIT)
         ]
 
-    tok_out = spread(tokens, tok_in, tok_s, tok_r)
-    cot_out = spread(cotangent, cot_in, cot_s, cot_r)
+    def by_clip(staging):
+        for n in range(0, width, step):
+            wide[...] = raw[:, :, pl.ds(n, step)].astype(F32)
+            for k in range(SPLIT):
+                staging[k, :, pl.ds(n, step)] = wide[:, k, :].astype(BF16)
+
+    tok_out = spread(staged, tok_in, tok_s, tok_r)
+    cot_out = spread(staged_grad, cot_in, cot_s, cot_r)
+    raw_tok.wait()
+    by_clip(staged)
+    raw_cot.start()
+    pl.semaphore_wait(barrier, SPLIT - 1 + GROUP - 1)
     for copy in tok_out:
         copy.start()
     for copy in weights:
         copy.start()
+    own_tok = pltpu.make_async_copy(staged.at[z], tok_in.at[z], tok_r.at[z])
+    own_tok.start()
+    raw_cot.wait()
+    by_clip(staged_grad)
+    own_cot = pltpu.make_async_copy(staged_grad.at[z], cot_in.at[z], cot_r.at[z])
+    own_cot.start()
+    for copy in small:
+        copy.wait()
 
     def wait_block(src, dst, send, recv, k):
         @pl.when(z == k)
@@ -146,10 +186,10 @@
     column = lax.broadcasted_iota(jnp.int32, (128, 128), 0)
     pick = jnp.where(column == index[:1], 1.0, 0.0)
     picks[...] = pick.astype(BF16)
-    tables[...] = jnp.zeros_like(tables)
-    tables[pl.ds(0, time_table.shape[0]), :] = time_table[...].astype(F32)
-    tables[pl.ds(TIMES, freq_table.shape[0]), :] = freq_table[...].astype(F32)
-    by_slot = dot(pick.T.astype(BF16), tables[...].astype(BF16)).astype(BF16)
+    pay[...] = jnp.zeros_like(pay)
+    pay[pl.ds(0, time_table.shape[0]), :] = time_table[...].astype(F32)
+    pay[pl.ds(TIMES, freq_table.shape[0]), :] = freq_table[...].astype(F32)
+    by_slot = dot(pick.T.astype(BF16), pay[...].astype(BF16)).astype(BF16)
 
     def slots_of(row_number, slot):
         block = sum((row_number >= padded * k).astype(jnp.int32) for k in range(1, SPLIT))
@@ -161,20 +201,32 @@
         return jnp.where(hit & (inside < rows) & (patch >= 0), 1.0, 0.0).astype(BF16)
 
     g1, s1 = row(gain1), row(shift1)
-    for k in range(SPLIT):
-        place = padded * k
+    bias_q, bias_v = qv_bias[0:1, :].astype(F32), qv_bias[1:2, :].astype(F32)
+    weights[0].wait()
+    for d in range(SPLIT):
+        k = (z, jnp.where(z % 2 == 0, z + 1, z - 1), jnp.where(z < 2, 2, 1), jnp.where(z < 2, 3, 0))[d]
+        place = pl.multiple_of(padded * k, 32)
+        block_rows = pl.ds(place, padded)
         number = lax.broadcasted_iota(jnp.int32, (padded, 128), 0) + place
         slot = lax.broadcasted_iota(jnp.int32, (padded, 128), 1)
         position = dot(slots_of(number, slot), by_slot)
-        wait_block(tokens, tok_in, tok_s, tok_r, k)
+        if d == 0:
+            own_tok.wait()
+        else:
+            remote(staged.at[k], tok_in.at[k], tok_s.at[0], tok_r.at[k], along(1)).wait_recv()
         stream_in[pl.ds(place, rows), :] = tok_in[k].astype(F32) + position[:rows]
         stream_in[pl.ds(place + rows, padded - rows), :] = jnp.zeros((padded - rows, width), F32)
-
-        @pl.loop(0, padded // 32)
-        def _(b):
-            at_row = pl.ds(pl.multiple_of(place + b * 32, 32), 32)
-            hat, _ = normalize(stream_in[at_row, :])
-            normed[at_row, :] = (hat * g1 + s1).astype(BF16)
+        hat, _ = normalize(stream_in[block_rows, :])
+        normed[block_rows, :] = (hat * g1 + s1).astype(BF16)
+        for t, (bias, scale) in enumerate(((bias_q, HDIM**-0.5), (None, 1.0), (bias_v, 1.0))):
+            for n in range(0, width, step):
+                part = dot(normed[block_rows, :], w_qkv[:, pl.ds(t * width + n, step)])
+                if bias is not None:
+                    part = part + bias[:, n : n + step]
+                part = part.astype(BF16)
+                if scale != 1.0:
+                    part = part * jnp.asarray(scale, BF16)
+                qkv[block_rows, pl.ds(t * width + n, step)] = part
 
     for copy in cot_out:
         copy.start()
@@ -188,8 +240,15 @@
                 left_out[i, q] = turned[1 - side]
 
     def left_copy(i):
+        if i >= 4:
+            return remote(
+                left_out.at[i], left.at[i, :, :, pl.ds(many, many)], left_s.at[i], left_r.at[i], at(1)
+            )
+        return left_quarter(i)
+
+    def left_quarter(q):
         return remote(
-            left_out.at[i], left.at[i, :, :, pl.ds(many, many)], left_s.at[i], left_r.at[i], at(1)
+            left_out.at[pl.ds(0, 4), q], left.at[pl.ds(0, 4), q, :, pl.ds(many, many)], left_s.at[q], left_r.at[q], at(1)
         )
 
     def hand_all(i, source):
@@ -203,18 +262,7 @@
             right.at[g, pl.ds(0, many)], right.at[g, pl.ds(many, many)], right_s.at[g], right_r.at[g], at(1)
         )
 
-    weights[0].wait()
     hand_all(6, normed)
-    bias_q, bias_v = qv_bias[0:1, :].astype(F32), qv_bias[1:2, :].astype(F32)
-    for t, (bias, scale) in enumerate(((bias_q, HDIM**-0.5), (None, 1.0), (bias_v, 1.0))):
-        for n in range(0, width, step):
-            part = dot(normed[...], w_qkv[:, pl.ds(t * width + n, step)])
-            if bias is not None:
-                part = part + bias[:, n : n + step]
-            part = part.astype(BF16)
-            if scale != 1.0:
-                part = part * jnp.asarray(scale, BF16)
-            qkv[:, pl.ds(t * width + n, step)] = part
 
     key_number = lax.broadcasted_iota(jnp.int32, (8, many), 1)
     key_block = sum((key_number >= padded * k).astype(jnp.int32) for k in range(1, SPLIT))
@@ -252,49 +300,61 @@
         )
     g2, s2 = row(gain2), row(shift2)
 
-    @pl.loop(0, many // 32)
+    @pl.loop(0, many // BLOCK)
     def _(b):
-        at_row = pl.ds(pl.multiple_of(b * 32, 32), 32)
+        at_row = pl.ds(pl.multiple_of(b * BLOCK, BLOCK), BLOCK)
         hat, _ = normalize(mid[at_row, :])
         normed[at_row, :] = (hat * g2 + s2).astype(BF16)
 
-    weights[2].wait()
-    hand_all(4, normed)
-    for q in range(4):
-        for n in range(0, width, step):
-            place = q * width + n
-            work[:, pl.ds(n, step)] = (
-                dot(normed[...], w_fc1[:, pl.ds(place, step)])
-                + fc1_bias[pl.ds(place, step)].astype(F32).reshape(1, step)
-            )
-
-        @pl.loop(0, many // 32)
-        def _(b):
-            at_row = pl.ds(pl.multiple_of(b * 32, 32), 32)
-            hidden = work[at_row, :]
+    def column_sums(value):
+        return jnp.sum(value.astype(F32), 0, keepdims=True)
+
+    def first_matrix(q, n):
+        place = pl.ds(pl.multiple_of(q * width + n, 128), step)
+        work[:, pl.ds(n, step)] = dot(normed[...], w_fc1[:, place]) + fc1_bias[place].astype(F32).reshape(1, step)
+
+    def activate(q, n):
+        for r in range(0, many, 64):
+            here = pl.ds(r, 64)
+            hidden = work[here, pl.ds(n, step)]
             cdf, pdf = normal_cdf_pdf(hidden)
-            unit[8 + q, at_row, :] = (hidden * cdf).astype(BF16)
-            right[1 + q, at_row, :] = (cdf + hidden * pdf).astype(BF16)
-
+            unit[8 + q, here, pl.ds(n, step)] = (hidden * cdf).astype(BF16)
+            right[1 + q, here, pl.ds(n, step)] = (cdf + hidden * pdf).astype(BF16)
+
+    def hand_quarter(q):
         turned = unit[8 + q].T.reshape(2, 4, shard, many)
         for u in range(4):
             hand_left(u, q, turned[:, u])
-
-    for u in range(4):
-        left_copy(u).start()
-
+        left_quarter(q).start()
+
+    weights[2].wait()
+    hand_all(4, normed)
+    first_matrix(0, 0)
+
+    def quarter(q, more):
+        for n in range(step, width, step):
+            first_matrix(q, n)
+            activate(q, n - step)
+        if more:
+            first_matrix(q + 1, 0)
+        activate(q, width - step)
+        hand_quarter(q)
+
+    @pl.loop(0, 3)
+    def _(q):
+        quarter(q, True)
+
+    wide_cot[pl.ds(rows, padded - rows), :] = jnp.zeros((padded - rows, step), F32)
     for k in range(SPLIT):
-        place = padded * k
-        wait_block(cotangent, cot_in, cot_s, cot_r, k)
-        work[pl.ds(place, rows), :] = cot_in[k].astype(F32)
-        work[pl.ds(place + rows, padded - rows), :] = jnp.zeros((padded - rows, width), F32)
-    right[0, pl.ds(0, many), :] = work[...].astype(BF16)
+        wait_block(staged_grad, cot_in, cot_s, cot_r, k)
+        for n in range(0, width, step):
+            wide_cot[pl.ds(0, rows), :] = cot_in[k, :, pl.ds(n, step)].astype(F32)
+            right[0, pl.ds(padded * k, padded), pl.ds(n, step)] = wide_cot[...].astype(BF16)
+    for n in range(0, width, step):
+        pay[pl.ds(99 + 7, 1), pl.ds(n, step)] = column_sums(right[0, pl.ds(0, many), pl.ds(n, step)])
     right_copy(0).start()
 
-    def column_sums(ref_value):
-        return jnp.sum(ref_value.astype(F32), 0, keepdims=True)
-
-    pay[pl.ds(99 + 7, 1), :] = column_sums(work[...])
+    quarter(3, False)
 
     A, B = pl.ds(0, half), pl.ds(half, half)
 
@@ -332,10 +392,12 @@
     def share_copy(i):
         return pltpu.make_async_copy(final.at[i], shares_hbm.at[i], share_s.at[i])
 
-    def product(i, l, g, first_left, first_right):
-        if first_left:
-            left_copy(l).wait_recv()
-        if first_right:
+    def product(i):
+        l = i if i < 4 else 4 if i < 8 else 5 if i == 8 else 6
+        g = 0 if i < 4 else i - 3
+        for other in range(4) if i == 0 else (l,) if i in (4, 8, 9) else ():
+            left_copy(other).wait_recv()
+        if i == 0 or i >= 4:
             right_copy(g).wait_recv()
         for n in range(0, width, step):
             part = dot(left[l].reshape(4 * shard, 2 * many), right[g, :, pl.ds(n, step)])
@@ -405,20 +467,10 @@
 
         share_copy(i).start()
 
-    ticks = (tick1, tick2, tick3, tick4, tick5)
-
-    def advance(n):
-        for k in range(len(ticks) - 1, -1, -1):
-            if 0 <= n - k < UNITS:
-                ticks[k](n - k)
-
-    for i in range(4):
-        product(i, i, 0, True, i == 0)
-
-    weights[3].wait()
-    bias = row(fc2_bias)
-    for n in range(0, width, step):
-        part = mid[:, pl.ds(n, step)] + bias[:, n : n + step]
+    bias_out = row(fc2_bias)
+
+    def block_out(n):
+        part = mid[:, pl.ds(n, step)] + bias_out[:, n : n + step]
         for q in range(4):
             part = part + dot(unit[8 + q], w_fc2[pl.ds(q * width, width), pl.ds(n, step)])
         for k in range(SPLIT):
@@ -432,9 +484,15 @@
         ]
 
     out_copies = give(staged, out_hbm, out_s, out_r)
-    for copy in out_copies:
-        copy.start()
-    advance(0)
+    grad_copies = give(staged_grad, grad_hbm, grad_s, grad_r)
+
+    def out_all():
+        for copy in tok_out:
+            copy.wait_send()
+        for n in range(0, width, step):
+            block_out(n)
+        for copy in out_copies:
+            copy.start()
 
     def grad_hidden(q):
         for n in range(0, width, step):
@@ -444,23 +502,13 @@
             pay[pl.ds(99 + 8 + q, 1), pl.ds(n, step)] = column_sums(part)
         right_copy(1 + q).start()
 
-    grad_hidden(0)
-    grad_hidden(1)
-    product(4, 4, 1, True, True)
-    product(5, 4, 2, False, True)
-    advance(1)
-    grad_hidden(2)
-    grad_hidden(3)
-    product(6, 4, 3, False, True)
-    product(7, 4, 4, False, True)
-    advance(2)
-
-    for n in range(0, width, step):
-        part = None
-        for q in range(4):
-            term = dot(right[1 + q, pl.ds(0, many), :], w_fc1[pl.ds(n, step), pl.ds(q * width, width)], NT)
-            part = term if part is None else part + term
-        work[:, pl.ds(n, step)] = part
+    def grad_second():
+        for n in range(0, width, step):
+            part = None
+            for q in range(4):
+                term = dot(right[1 + q, pl.ds(0, many), :], w_fc1[pl.ds(n, step), pl.ds(q * width, width)], NT)
+                part = term if part is None else part + term
+            work[:, pl.ds(n, step)] = part
 
     def norm_back(grad, value, gain):
         hat, rstd = normalize(value)
@@ -470,31 +518,32 @@
 
     zero = jnp.zeros((1, width), F32)
 
-    def back_second(b, sums):
-        at_row = pl.ds(pl.multiple_of(b * 32, 32), 32)
-        grad = work[at_row, :]
-        back, hat = norm_back(grad, mid[at_row, :], g2)
-        back = back + right[0, at_row, :].astype(F32)
-        mid[at_row, :] = back
-        branch = back.astype(BF16)
-        right[5, at_row, :] = branch
-        return (
-            sums[0] + column_sums(grad * hat),
-            sums[1] + column_sums(grad),
-            sums[2] + column_sums(branch),
-        )
-
-    sums = lax.fori_loop(0, many // 32, back_second, (zero, zero, zero))
-    pay[pl.ds(99 + 5, 1), :] = sums[0]
-    pay[pl.ds(99 + 6, 1), :] = sums[1]
-    pay[pl.ds(99 + 4, 1), :] = sums[2]
-    right_copy(5).start()
-    for n in range(0, width, step):
-        normed[:, pl.ds(n, step)] = dot(
-            right[5, pl.ds(0, many), :], w_proj[pl.ds(n, step), :], NT
-        ).astype(BF16)
-    product(8, 5, 5, True, True)
-    advance(3)
+    def second_norm():
+        def block(b, sums):
+            at_row = pl.ds(pl.multiple_of(b * BLOCK, BLOCK), BLOCK)
+            grad = work[at_row, :]
+            back, hat = norm_back(grad, mid[at_row, :], g2)
+            back = back + right[0, at_row, :].astype(F32)
+            mid[at_row, :] = back
+            branch = back.astype(BF16)
+            right[5, at_row, :] = branch
+            return (
+                sums[0] + column_sums(grad * hat),
+                sums[1] + column_sums(grad),
+                sums[2] + column_sums(branch),
+            )
+
+        sums = lax.fori_loop(0, many // BLOCK, block, (zero, zero, zero))
+        pay[pl.ds(99 + 5, 1), :] = sums[0]
+        pay[pl.ds(99 + 6, 1), :] = sums[1]
+        pay[pl.ds(99 + 4, 1), :] = sums[2]
+        right_copy(5).start()
+
+    def grad_attended():
+        for n in range(0, width, step):
+            normed[:, pl.ds(n, step)] = dot(
+                right[5, pl.ds(0, many), :], w_proj[pl.ds(n, step), :], NT
+            ).astype(BF16)
 
     def attend_back(p):
         query, key, value = (qkv[:, lanes(t, p)] for t in range(3))
@@ -518,64 +567,49 @@
             if t != 1:
                 pay[pl.ds(99 + 2 + t // 2, 1), lanes(0, p)] = column_sums(low_grad)
 
-    parts = 3
-    for s in range(parts):
-        @pl.loop(s * pairs // parts, (s + 1) * pairs // parts)
+    def attention_back(s):
+        @pl.loop(s * pairs // 3, (s + 1) * pairs // 3)
         def _(p):
             attend_back(p)
 
-        if s < parts - 1:
-            advance(4 + s)
-    for t in range(3):
-        right_copy(6 + t).start()
-    for t in range(3):
-        product(9 + t, 6, 6 + t, t == 0, True)
-    advance(6)
-
-    for n in range(0, width, step):
-        part = None
-        for t in range(3):
-            term = dot(right[6 + t, pl.ds(0, many), :], w_qkv[pl.ds(n, step), pl.ds(t * width, width)], NT)
-            part = term if part is None else part + term
-        work[:, pl.ds(n, step)] = part
-
-    def back_first(b, sums):
-        at_row = pl.ds(pl.multiple_of(b * 32, 32), 32)
-        grad = work[at_row, :]
-        back, hat = norm_back(grad, stream_in[at_row, :], g1)
-        mid[at_row, :] = mid[at_row, :] + back
-        return sums[0] + column_sums(grad * hat), sums[1] + column_sums(grad)
-
-    sums = lax.fori_loop(0, many // 32, back_first, (zero, zero))
-    pay[pl.ds(99, 1), :] = sums[0]
-    pay[pl.ds(100, 1), :] = sums[1]
-    for k in range(SPLIT):
-        staged_grad[k] = mid[pl.ds(padded * k, padded), :][:rows].astype(BF16)
-    grad_copies = give(staged_grad, grad_hbm, grad_s, grad_r)
-    for copy in grad_copies:
-        copy.start()
+        if s == 2:
+            for t in range(3):
+                right_copy(6 + t).start()
+
+    def grad_first():
+        for n in range(0, width, step):
+            part = None
+            for t in range(3):
+                term = dot(right[6 + t, pl.ds(0, many), :], w_qkv[pl.ds(n, step), pl.ds(t * width, width)], NT)
+                part = term if part is None else part + term
+            work[:, pl.ds(n, step)] = part
+
+    def first_norm():
+        def block(b, sums):
+            at_row = pl.ds(pl.multiple_of(b * BLOCK, BLOCK), BLOCK)
+            grad = work[at_row, :]
+            back, hat = norm_back(grad, stream_in[at_row, :], g1)
+            mid[at_row, :] = mid[at_row, :] + back
+            return sums[0] + column_sums(grad * hat), sums[1] + column_sums(grad)
+
+        sums = lax.fori_loop(0, many // BLOCK, block, (zero, zero))
+        pay[pl.ds(99, 1), :] = sums[0]
+        pay[pl.ds(100, 1), :] = sums[1]
+        for copy in cot_out:
+            copy.wait_send()
+        for k in range(SPLIT):
+            staged_grad[k] = mid[pl.ds(padded * k, padded), :][:rows].astype(BF16)
+        for copy in grad_copies:
+            copy.start()
 
     def halves(v):
         high = v.astype(BF16)
         return high, (v - high.astype(F32)).astype(BF16)
 
-    number = lax.broadcasted_iota(jnp.int32, (128, many), 1)
-    slot = lax.broadcasted_iota(jnp.int32, (128, many), 0)
-    slots = slots_of(number, slot)
-    for n in range(0, width, step):
-        by = sum(dot(slots, v) for v in halves(mid[:, pl.ds(n, step)]))
-        table_grad = sum(dot(picks[...], v) for v in halves(by))
-        pay[pl.ds(0, 99), pl.ds(n, step)] = table_grad[:99]
-        pay[pl.ds(TIMES, 16), pl.ds(n, step)] = table_grad[TIMES:]
-    pay[pl.ds(111, 1), :] = zero
-
     def pay_copy(bits):
-        return remote(pay.at[pl.ds(16 * peer(bits), 16)], pay_in.at[low], pay_s.at[bits - 1], pay_r.at[low], at(bits))
-
-    def pay_wait(bits):
-        remote(
-            pay.at[pl.ds(0, 16)], pay_in.at[peer(bits)], pay_s.at[bits - 1], pay_r.at[peer(bits)], at(bits)
-        ).wait_recv()
+        return remote(
+            pay_low.at[pl.ds(16 * peer(bits), 16)], pay_in.at[low], pay_s.at[bits - 1], pay_r.at[low], at(bits)
+        )
 
     def payz_copy(d):
         return remote(pay_mid.at[z], pay_mid.at[z], payz_s.at[d - 1], payz_r.at[z], along(d))
@@ -583,24 +617,54 @@
     def payo_copy(bits):
         return remote(pay_out.at[low], pay_out.at[low], payo_s.at[bits - 1], payo_r.at[low], at(bits))
 
-    for bits in range(1, GROUP):
-        pay_copy(bits).start()
-    advance(7)
-    for bits in range(1, GROUP):
-        pay_wait(bits)
-    pay_in[low] = pay[pl.ds(pl.multiple_of(16 * low, 16), 16), :]
-    pay_mid[z] = sum(pay_in[s] for s in range(GROUP))
-    for d in range(1, SPLIT):
-        payz_copy(d).start()
-    advance(8)
-    for d in range(1, SPLIT):
-        k = (z + d) % SPLIT
-        remote(pay_mid.at[k], pay_mid.at[k], payz_s.at[d - 1], payz_r.at[k], along(d)).wait_recv()
-    pay_out[low] = sum(pay_mid[s] for s in range(SPLIT))
-    for bits in range(1, GROUP):
-        payo_copy(bits).start()
-    for n in range(9, UNITS + len(ticks) - 1):
-        advance(n)
+    def position_tables():
+        number = lax.broadcasted_iota(jnp.int32, (128, many), 1)
+        slot = lax.broadcasted_iota(jnp.int32, (128, many), 0)
+        slots = slots_of(number, slot)
+        for n in range(0, width, step):
+            by = sum(dot(slots, v) for v in halves(mid[:, pl.ds(n, step)]))
+            table_grad = sum(dot(picks[...], v) for v in halves(by))
+            pay[pl.ds(0, 99), pl.ds(n, step)] = table_grad[:99]
+            pay[pl.ds(TIMES, 16), pl.ds(n, step)] = table_grad[TIMES:]
+        pay[pl.ds(111, 1), :] = zero
+        pay_low[...] = pay[...].astype(BF16)
+        for bits in range(1, GROUP):
+            pay_copy(bits).start()
+
+    def pay_group():
+        for bits in range(1, GROUP):
+            remote(
+                pay_low.at[pl.ds(0, 16)], pay_in.at[peer(bits)], pay_s.at[bits - 1], pay_r.at[peer(bits)], at(bits)
+            ).wait_recv()
+        pay_in[low] = pay_low[pl.ds(pl.multiple_of(16 * low, 16), 16), :]
+        pay_mid[z] = sum(pay_in[s].astype(F32) for s in range(GROUP)).astype(BF16)
+        for d in range(1, SPLIT):
+            payz_copy(d).start()
+
+    def pay_line():
+        for d in range(1, SPLIT):
+            k = (z + d) % SPLIT
+            remote(pay_mid.at[k], pay_mid.at[k], payz_s.at[d - 1], payz_r.at[k], along(d)).wait_recv()
+        pay_out[low] = sum(pay_mid[s].astype(F32) for s in range(SPLIT)).astype(BF16)
+        for bits in range(1, GROUP):
+            payo_copy(bits).start()
+
+    pieces = {
+        "out": out_all, "sec": grad_second, "sen": second_norm, "att": grad_attended, "fir": grad_first,
+        "fin": first_norm, "tab": position_tables, "pay2": pay_group, "pay3": pay_line,
+    }
+    for q in range(4):
+        pieces[f"gh{q}"] = functools.partial(grad_hidden, q)
+    for s in range(3):
+        pieces[f"ab{s}"] = functools.partial(attention_back, s)
+    for i in range(UNITS):
+        pieces[f"t0_{i}"] = functools.partial(product, i)
+        for k, tick in enumerate((tick1, tick2, tick3, tick4, tick5)):
+            pieces[f"t{k + 1}_{i}"] = functools.partial(tick, i)
+    assert sorted(ORDER) == sorted(pieces)
+    weights[3].wait()
+    for name in ORDER:
+        pieces[name]()
     for bits in range(1, GROUP):
         remote(
             pay_out.at[low], pay_out.at[peer(bits)], payo_s.at[bits - 1], payo_r.at[peer(bits)], at(bits)
@@ -608,7 +672,7 @@
     last = pltpu.make_async_copy(pay_out, small_hbm, w_sem.at[0])
     last.start()
 
-    for copies in (tok_out, cot_out, out_copies[1:], grad_copies[1:]):
+    for copies in (out_copies[1:], grad_copies[1:]):
         for copy in copies:
             copy.wait_send()
     for k in range(SPLIT):
@@ -645,12 +709,72 @@
     last.wait()
 
 
+def finish_kernel(
+    out_in, grad_in, shares, small,
+    out, grad, freq, time, gain1, shift1, qkv, qv_bias, proj, proj_bias, gain2, shift2, fc1, fc1_bias, fc2, fc2_bias,
+    rows_in, wide, rows_out, parts, small_in, f_qkv, f_proj, f_fc1, f_fc2, f_time, f_freq, f_qv, lines,
+    row_sem, part_sem, out_sem,
+):
+    width = wide.shape[2]
+    shard = parts.shape[1]
+    reads = [pltpu.make_async_copy(shares.at[i], parts.at[i], part_sem.at[i]) for i in range(UNITS)]
+    moves = [pltpu.make_async_copy(src, rows_in.at[i], row_sem.at[i]) for i, src in enumerate((out_in, grad_in))]
+    read_small = pltpu.make_async_copy(small, small_in, row_sem.at[2])
+    for copy in (*reads, *moves, read_small):
+        copy.start()
+    line_of = lambda i: lines.at[pl.ds(i * width, width)]
+    writes = [
+        pltpu.make_async_copy(src, dst, out_sem.at[i])
+        for i, (src, dst) in enumerate(
+            (
+                (f_fc2, fc2), (f_fc1, fc1), (f_proj, proj), (f_qkv, qkv), (rows_out.at[0], out), (rows_out.at[1], grad),
+                (f_time, time), (f_freq, freq), (f_qv, qv_bias), (line_of(0), gain1), (line_of(1), shift1),
+                (line_of(2), proj_bias), (line_of(3), gain2), (line_of(4), shift2), (line_of(5), fc2_bias),
+                (lines.at[pl.ds(6 * width, 4 * width)], fc1_bias),
+            )
+        )
+    ]
+    for i in range(UNITS):
+        reads[i].wait()
+        value = parts[i].astype(F32)
+        if i < 4:
+            f_fc2[pl.ds(i * shard, shard), :] = value
+        elif i < 8:
+            f_fc1[:, pl.ds((i - 4) * width, width)] = value
+        elif i == 8:
+            f_proj[...] = value
+        else:
+            f_qkv[:, pl.ds((i - 9) * width, width)] = value
+        if i in (3, 7, 8, 11):
+            writes[(3, 7, 8, 11).index(i)].start()
+    for i in range(2):
+        moves[i].wait()
+        for k in range(SPLIT):
+            wide[:, k, :] = rows_in[i, k].astype(F32)
+        rows_out[i] = wide[...].astype(BF16)
+        writes[4 + i].start()
+    read_small.wait()
+    f_time[...] = small_in[pl.ds(0, time.shape[0]), :].astype(F32)
+    f_freq[...] = small_in[pl.ds(TIMES, freq.shape[0]), :].astype(F32)
+    rest = small_in[pl.ds(96, 16), :].astype(F32)[3:]
+    f_qv[...] = rest[2:4]
+    for at, i in enumerate((0, 1, 4, 5, 6, 7)):
+        lines[pl.ds(at * width, width)] = rest[i : i + 1].reshape(width)
+    for q in range(4):
+        lines[pl.ds((6 + q) * width, width)] = rest[8 + q : 9 + q].reshape(width)
+    for copy in writes[6:]:
+        copy.start()
+    for copy in writes:
+        copy.wait()
+
+
 def on_device(
     tokens, freq_index, time_index, freq_table, time_table,
     norm1_gain, norm1_shift, qkv_weight, qv_bias, proj_weight, proj_bias, norm2_gain, norm2_shift,
     fc1_weight, fc1_bias, fc2_weight, fc2_bias, cotangent,
 ):
     clips, rows, width = tokens.shape
+    times, freqs = time_table.shape[0], freq_table.shape[0]
     groups = lax.axis_size("seq")
     clip_devices = lax.axis_size("clip")
     assert clips == SPLIT and groups == SPLIT and clip_devices % GROUP == 0
@@ -662,31 +786,34 @@
     half = width // 2
     heads = width // HDIM
 
-    vmem = pl.BlockSpec(memory_space=pltpu.VMEM)
-    smem = pl.BlockSpec(memory_space=pltpu.SMEM)
     anywhere = pl.BlockSpec(memory_space=pl.ANY)
     dma = pltpu.SemaphoreType.DMA
     blocks = (SPLIT, rows, width)
+    vectors = (freq_table, time_table, norm1_gain, norm1_shift, qv_bias, proj_bias, norm2_gain, norm2_shift, fc1_bias, fc2_bias)
+    small_scratch = [pltpu.SMEM(v.shape, v.dtype) for v in (freq_index, time_index)]
+    small_scratch += [pltpu.VMEM(v.shape, v.dtype) for v in vectors]
+    tokens, cotangent = (v.transpose(1, 0, 2) for v in (tokens, cotangent))
     out, grad, shares, small = pl.pallas_call(
         block_kernel,
         out_shape=(
             jax.ShapeDtypeStruct(blocks, BF16),
             jax.ShapeDtypeStruct(blocks, BF16),
             jax.ShapeDtypeStruct((UNITS, shard, width), BF16),
-            jax.ShapeDtypeStruct((GROUP, 16, width), F32),
+            jax.ShapeDtypeStruct((GROUP, 16, width), BF16),
         ),
-        in_specs=[
-            anywhere, smem, smem, vmem, vmem, vmem, vmem, anywhere, vmem, anywhere, vmem, vmem, vmem,
-            anywhere, vmem, anywhere, vmem, anywhere,
-        ],
+        in_specs=[anywhere] * 18,
         out_specs=(anywhere,) * 4,
         scratch_shapes=[
+            *small_scratch,
+            pltpu.VMEM((rows, SPLIT, width), BF16),
+            pltpu.VMEM((rows, SPLIT, 256 if width % 256 == 0 else 128), F32),
             pltpu.VMEM((width, 3 * width), BF16),
             pltpu.VMEM((width, width), BF16),
             pltpu.VMEM((width, hidden_width), BF16),
             pltpu.VMEM((hidden_width, width), BF16),
             pltpu.VMEM(blocks, BF16),
             pltpu.VMEM(blocks, BF16),
+            pltpu.VMEM((padded, 256 if width % 256 == 0 else 128), F32),
             pltpu.VMEM((many, width), F32),
             pltpu.VMEM((many, width), BF16),
             pltpu.VMEM((many, 3 * width), BF16),
@@ -705,13 +832,13 @@
             pltpu.VMEM((UNITS, shard, width), BF16),
             pltpu.VMEM(blocks, BF16),
             pltpu.VMEM(blocks, BF16),
-            pltpu.VMEM((128, width), F32),
             pltpu.VMEM((128, 128), BF16),
             pltpu.VMEM((128, width), F32),
-            pltpu.VMEM((GROUP, 16, width), F32),
-            pltpu.VMEM((SPLIT, 16, width), F32),
-            pltpu.VMEM((GROUP, 16, width), F32),
-            dma((4,)),
+            pltpu.VMEM((128, width), BF16),
+            pltpu.VMEM((GROUP, 16, width), BF16),
+            pltpu.VMEM((SPLIT, 16, width), BF16),
+            pltpu.VMEM((GROUP, 16, width), BF16),
+            dma((12,)), dma((2,)), dma((4,)),
             dma((3,)), dma((4,)), dma((3,)), dma((4,)), dma((3,)), dma((4,)), dma((3,)), dma((4,)),
             dma((7,)), dma((7,)), dma((9,)), dma((9,)),
             dma((UNITS, 2)), dma((UNITS, 2)), dma((UNITS, 2)), dma((UNITS, 2)),
@@ -727,29 +854,58 @@
         norm1_gain, norm1_shift, qkv_weight, qv_bias, proj_weight, proj_bias, norm2_gain, norm2_shift,
         fc1_weight, fc1_bias, fc2_weight, fc2_bias, cotangent,
     )
-    shares = shares.astype(F32)
     small = small.reshape(GROUP * 16, width)
-    if clip_devices > GROUP:
-        count = clip_devices // GROUP
-        same = [[h * GROUP + b for h in range(count)] for b in range(GROUP)]
-        small = lax.psum(small, "clip", axis_index_groups=same)
-        fc2 = shares[:4].reshape(4 * shard, width)
-        rest = shares[4:].transpose(1, 0, 2).reshape(shard, 8 * width)
-        summed = [
-            lax.psum_scatter(v, "clip", scatter_dimension=0, axis_index_groups=same, tiled=True)
-            for v in (fc2, rest)
-        ]
-        moves = [(h * GROUP + b, b * count + h) for h in range(count) for b in range(GROUP)]
-        fc2, rest = (lax.ppermute(v, "clip", moves) for v in summed)
-    else:
-        fc2 = shares[:4].reshape(4 * shard, width)
-        rest = shares[4:].transpose(1, 0, 2).reshape(shard, 8 * width)
+    if clip_devices == GROUP:
+        shape = lambda *dims: jax.ShapeDtypeStruct(dims, F32)
+        inner = jax.ShapeDtypeStruct((rows, SPLIT, width), BF16)
+        line = shape(width)
+        results = (
+            inner, inner, shape(freqs, width), shape(times, width), line, line, shape(shard, 3 * width),
+            shape(2, width), shape(shard, width), line, line, line, shape(shard, 4 * width),
+            shape(4 * width), shape(4 * shard, width), line,
+        )
+        out, grad, *others = pl.pallas_call(
+            finish_kernel,
+            out_shape=results,
+            in_specs=[anywhere] * 4,
+            out_specs=(anywhere,) * 16,
+            scratch_shapes=[
+                pltpu.VMEM((2, *blocks), BF16),
+                pltpu.VMEM((rows, SPLIT, width), F32),
+                pltpu.VMEM((2, rows, SPLIT, width), BF16),
+                pltpu.VMEM((UNITS, shard, width), BF16),
+                pltpu.VMEM((GROUP * 16, width), BF16),
+                pltpu.VMEM((shard, 3 * width), F32),
+                pltpu.VMEM((shard, width), F32),
+                pltpu.VMEM((shard, 4 * width), F32),
+                pltpu.VMEM((4 * shard, width), F32),
+                pltpu.VMEM((times, width), F32),
+                pltpu.VMEM((freqs, width), F32),
+                pltpu.VMEM((2, width), F32),
+                pltpu.VMEM((10 * width,), F32),
+                dma((3,)), dma((UNITS,)), dma((16,)),
+            ],
+            compiler_params=pltpu.CompilerParams(vmem_limit_bytes=62 * 2**20),
+        )(out, grad, shares, small)
+        return (out.transpose(1, 0, 2), grad.transpose(1, 0, 2), *others)
+    shares, small = shares.astype(F32), small.astype(F32)
+    count = clip_devices // GROUP
+    same = [[h * GROUP + b for h in range(count)] for b in range(GROUP)]
+    small = lax.psum(small, "clip", axis_index_groups=same)
+    fc2 = shares[:4].reshape(4 * shard, width)
+    rest = shares[4:].transpose(1, 0, 2).reshape(shard, 8 * width)
+    summed = [
+        lax.psum_scatter(v, "clip", scatter_dimension=0, axis_index_groups=same, tiled=True)
+        for v in (fc2, rest)
+    ]
+    moves = [(h * GROUP + b, b * count + h) for h in range(count) for b in range(GROUP)]
+    fc2, rest = (lax.ppermute(v, "clip", moves) for v in summed)
     fc1, proj, qkv = rest[:, : 4 * width], rest[:, 4 * width : 5 * width], rest[:, 5 * width :]
     return (
         out,
         grad,
-        small[TIMES : TIMES + freq_table.shape[0]],
-        small[: time_table.shape[0]],
+        small[TIMES : TIMES + freqs],
+        small[:times],
         small[99],
         small[100],
         qkv,

time: 184 us -> 135 us (0.73)
  Pallas kernels: 162 us -> 134 us
  local copies, waits for them, and re-layouts: 20.3 us -> 0 us
    pallas_call x1, Pallas kernels: 162 us -> 130 us  [on_device(): pl.pallas_call(block_kernel, out_shape=(jax.ShapeDtypeStruct(blocks, BF16...]
    slice x9 -> x0, local copies, waits for them, and re-layouts: 10.6 us -> none  [the longest x1 1.71 us: on_device(): small[:time_table.shape[0]]]
    unnamed x7 -> x0, local copies, waits for them, and re-layouts: 8.82 us -> none
    pallas_call x0 -> x1, Pallas kernels: none -> 4.02 us  [on_device(): pl.pallas_call(finish_kernel, out_shape=results, in_specs=[anywhere] * 4,...]
where the time goes in v2:
time: 135 us
  Pallas kernels  134 us (99%)
    pallas_call x1, Pallas kernels, on_device(): pl.pallas_call(block_kernel, out_shape=(jax.ShapeDtypeStruct(blocks, BF16...  130 us
    pallas_call x1, Pallas kernels, on_device(): pl.pallas_call(finish_kernel, out_shape=results, in_specs=[anywhere] * 4,...  4.02 us

profile of v2, /device:TPU:0, one launch (start us, length us, event | category | flops | bytes accessed | tf_op | source)
XLA Modules:
  0.0 135.1 jit_solution(15712107976644290720)
XLA Ops:
  0.7 130.2 %shard_map.297 = (bf16[4,95,768]{2,1,0:T(8,128)(2,1)}, bf16[4,95,768]{2,1,0:T(8,128)(2,1)}, bf16[12,96,768]{2,1,0:T(8,128)(2,1)}, bf16[8,16,768]{2,1,0:T(8,128)(2,1)}) custom-call(bf16[95,4,768]{2,1,0:T(4,128)(2,1)} %bitcast.5, s32[4,7]{1,0:T(4,128)} %freq_index_hbm.1, s32[4,54]{1,0:T(4,128)} %time_index_hbm.1, bf16[12,768]{1,0:T(8,128)(2,1)} %freq_table_hbm.1, ...), custom_call_target="tpu_custom_call" | custom-call | tf_op jit(solution)/shard_map/pallas_call | solution.py:796
  130.9 4.0 %shard_map.298 = (bf16[95,4,768]{2,1,0:T(4,128)(2,1)}, bf16[95,4,768]{2,1,0:T(4,128)(2,1)}, f32[12,768]{1,0:T(8,128)}, f32[99,768]{1,0:T(8,128)}, f32[768]{0:T(1...) custom-call(bf16[4,95,768]{2,1,0:T(8,128)(2,1)} %get-tuple-element.3, ...), custom_call_target="tpu_custom_call" | custom-call | tf_op jit(solution)/shard_map/pallas_call | solution.py:867
